TPU v7x, 1024 devices: a whole 8x8x8 slice. The times are simulated.
1024 devices in a mesh: band: 32 (over z_lo, y, core), ga: 32 (over z_hi, x).
Axes of the slice: x: 8, y: 8, z: 8 (z_hi: 4, z_lo: 2; z = z_hi * 2 + z_lo), core: 2. Of those that a mesh axis runs over, the one named last changes fastest.
Arguments:
- psi: float32 [1024, 196608], P('band', 'ga'), may hold values from -0.084712684 to 0.084712684
- hpsi: float32 [1024, 196608], P('band', 'ga'), may hold values from -6 to 6
Outputs:
- residual: float32 [1024, 196608], P('band', 'ga')
All inputs are finite; a program needn't handle non-finite values.
Results may differ from a plain program's by a relative error of at most 0.0001.
Values sent between devices are 32-bit elements; how exact they have to be, the bound alone decides.
No kernel may reach another device: no remote copies, remote signals or barrier semaphores. Data moves between devices by JAX's collectives and lax.ppermute only.
A program may use at most 32 MiB of HBM per device.

v0:
```python
import jax
import jax.numpy as jnp
from jax import lax
from jax.sharding import PartitionSpec as P

STEPS = 4


def from_behind(value, axis, steps):
    count = lax.axis_size(axis)
    pairs = [(source, (source + steps) % count) for source in range(count)]
    return lax.ppermute(value, axis, pairs)


def on_device(psi, hpsi):
    blocks = [psi]
    current = psi
    for step in range(STEPS - 1):
        current = from_behind(current, "band", 1)
        blocks.append(current)
    window = jnp.concatenate(blocks, 0)
    partial_intersection = lax.dot_general(
        window,
        hpsi,
        (((1,), (1,)), ((), ())),
        precision=lax.Precision.HIGHEST,
        preferred_element_type=jnp.float32,
    )
    intersection = lax.psum(partial_intersection, "ga")
    projected = lax.dot_general(
        intersection,
        window,
        (((0,), (0,)), ((), ())),
        precision=lax.Precision.HIGHEST,
        preferred_element_type=jnp.float32,
    )
    return hpsi - projected


def solution(mesh):
    placed = (P("band", "ga"), P("band", "ga"))
    return jax.shard_map(
        on_device, mesh=mesh, in_specs=placed, out_specs=P("band", "ga"), check_vma=False
    )
```

profile of v0, /device:TPU:128, one launch (start us, length us, event | category | flops | bytes accessed | tf_op | source)
XLA Modules:
  0.0 220.9 jit_solution(13573922843487398940)
XLA Ops:
  0.0 0.0 copy-start
  0.0 2.0 collective-permute-start
  2.0 13.7 %collective-permute-done = f32[32,6144]{1,0:T(8,128)S(1)} collective-permute-done((f32[32,6144]{1,0:T(8,128)}, f32[32,6144]{1,0:T(8,128)S(1)}, u32[]{:S(2)}, u32[]{:S(2)}) %collective-permute-start) | collective-permute-done | bytes 786464 | tf_op jit(solution)/shard_map/ppermute | solution.py:12
  15.8 1.9 collective-permute-start.1
  17.7 1.2 constant_dynamic-update-slice_fusion.3
  18.9 12.3 %collective-permute-done.1 = f32[32,6144]{1,0:T(8,128)S(1)} collective-permute-done((f32[32,6144]{1,0:T(8,128)S(1)}, f32[32,6144]{1,0:T(8,128)S(1)}, u32[]{:S(2)}, u32[]{:S(2)}) %collective-permute-start.1) | collective-permute-done | bytes 786464 | tf_op jit(solution)/shard_map/ppermute | solution.py:12
  31.2 1.9 collective-permute-start.2
  33.1 0.1 constant_dynamic-update-slice_fusion.2
  33.1 0.1 constant_dynamic-update-slice_fusion.1
  33.2 13.4 %collective-permute-done.2 = f32[32,6144]{1,0:T(8,128)S(1)} collective-permute-done((f32[32,6144]{1,0:T(8,128)S(1)}, f32[32,6144]{1,0:T(8,128)S(1)}, u32[]{:S(2)}, u32[]{:S(2)}) %collective-permute-start.2) | collective-permute-done | bytes 786464 | tf_op jit(solution)/shard_map/ppermute | solution.py:12
  46.6 0.1 constant_dynamic-update-slice_fusion
  46.6 0.0 copy-done
  46.6 2.6 %fusion = f32[128,32]{1,0:T(8,128)S(1)} fusion(f32[128,6144]{1,0:T(8,128)S(1)} %constant_dynamic-update-slice_fusion, f32[32,6144]{1,0:T(8,128)S(1)} %copy-done), kind=kOutput, calls=%fused_computation.5 | convolution fusion | flops 301989888 | bytes 3948544 | tf_op jit(solution)/shard_map/dot_general | solution.py:22
  49.2 167.9 %psum.7 = f32[128,32]{1,0:T(8,128)S(1)} all-reduce(f32[128,32]{1,0:T(8,128)S(1)} %fusion), channel_id=1, replica_groups=mesh['band'=32,'ga'=32] {'ga'}, use_global_device_ids=true, to_apply=%region_0.0 | all-reduce | flops 4096 | bytes 32768 | tf_op jit(solution)/shard_map/psum | solution.py:29
  217.2 3.7 %convolution_subtract_fusion = f32[32,6144]{1,0:T(8,128)} fusion(f32[32,6144]{1,0:T(8,128)} %param.3, f32[128,32]{1,0:T(8,128)S(1)} %psum.7, f32[128,6144]{1,0:T(8,128)S(1)} %constant_dynamic-update-slice_fusion), kind=kOutput, calls=%fused_computation | convolution fusion | flops 302186496 | bytes 4734976 | tf_op jit(solution)/shard_map/dot_general | solution.py:30
Async XLA Ops:
  0.0 46.6 %copy-start = (f32[32,6144]{1,0:T(8,128)S(1)}, f32[32,6144]{1,0:T(8,128)}, u32[]{:S(2)}) copy-start(f32[32,6144]{1,0:T(8,128)} %param.3) | copy-start | bytes 2359300
  0.0 15.7 %collective-permute-start = (f32[32,6144]{1,0:T(8,128)}, f32[32,6144]{1,0:T(8,128)S(1)}, u32[]{:S(2)}, u32[]{:S(2)}) collective-permute-start(f32[32,6144]{1,0:T(8,128)} %param.2), channel_id=1, source_target_pairs={{0,32},{32,64},{64,96},{96,128},{128,160},{160,192},{192,224},{224... | collective-permute-start | bytes 2359304 | tf_op jit(solution)/shard_map/ppermute | solution.py:12
  15.8 15.4 %collective-permute-start.1 = (f32[32,6144]{1,0:T(8,128)S(1)}, f32[32,6144]{1,0:T(8,128)S(1)}, u32[]{:S(2)}, u32[]{:S(2)}) collective-permute-start(f32[32,6144]{1,0:T(8,128)S(1)} %collective-permute-done), channel_id=1, source_target_pairs={{0,32},{32,64},{64,96},{96,128},{128,160},{160,192},{192,224},{224... | collective-permute-start | bytes 2359304 | tf_op jit(solution)/shard_map/ppermute | solution.py:12
  31.2 15.4 %collective-permute-start.2 = (f32[32,6144]{1,0:T(8,128)S(1)}, f32[32,6144]{1,0:T(8,128)S(1)}, u32[]{:S(2)}, u32[]{:S(2)}) collective-permute-start(f32[32,6144]{1,0:T(8,128)S(1)} %collective-permute-done.1), channel_id=1, source_target_pairs={{0,32},{32,64},{64,96},{96,128},{128,160},{160,192},{192,224},{224... | collective-permute-start | bytes 2359304 | tf_op jit(solution)/shard_map/ppermute | solution.py:12
where the time goes:
time: 221 us
  blocking collectives  168 us (76%)
  waiting for transfers between devices  39.4 us (18%)
  matrix products  6.29 us (3%)
  starting transfers between devices  5.86 us (3%)
    psum x1, blocking collectives, on_device(): intersection = lax.psum(partial_intersection, 'ga')  168 us
    ppermute x3, waiting for transfers between devices, from_behind(): return lax.ppermute(value, axis, pairs)  39.4 us
    ppermute x3, starting transfers between devices, from_behind(): return lax.ppermute(value, axis, pairs)  5.86 us
  transfers between devices with their start and end apart: 3, of which 3 were waited for; matrix products, arithmetic and copies ran while one was open for 1% of the time, Pallas kernels for 0%

commit v1 on v0

v1 whole, which is shorter than its diff:
```python
import jax
import jax.numpy as jnp
from jax import lax
from jax.sharding import Mesh, PartitionSpec as P

BAND = ("zl", "y", "core")
GA = ("zh", "x")
PRECISION = lax.Precision.HIGH


def shifted(value, steps):
    count = lax.axis_size(BAND)
    pairs = [(source, (source + steps) % count) for source in range(count)]
    return lax.ppermute(value, BAND, pairs)


def swapped(value):
    return lax.ppermute(value, "core", [(0, 1), (1, 0)])


def overlap(h, psi):
    return lax.dot_general(
        h, psi, (((1,), (1,)), ((), ())), precision=PRECISION, preferred_element_type=jnp.float32
    )


def project(inter, psi):
    return lax.dot_general(
        inter, psi, (((1,), (0,)), ((), ())), precision=PRECISION, preferred_element_type=jnp.float32
    )


def summed(partial):
    count = lax.axis_size(GA)
    copies = jnp.broadcast_to(partial[None], (count,) + partial.shape)
    return jnp.sum(lax.all_to_all(copies, GA, 0, 0, tiled=True), 0)


def on_device(psi, hpsi):
    odd = lax.axis_index("core") == 1
    behind2 = shifted(psi, 2)
    ahead1 = shifted(hpsi, -1)
    for_next = jnp.concatenate([overlap(ahead1, psi), overlap(ahead1, behind2)], 1)
    from_previous = shifted(for_next, 1)
    own = jnp.concatenate([overlap(hpsi, psi), overlap(hpsi, behind2)], 1)
    inter = summed(jnp.concatenate([own, from_previous], 1))
    behind1 = swapped(jnp.where(odd, behind2, psi))
    behind3 = shifted(behind2, 1)
    window = jnp.concatenate([psi, behind2, behind1, behind3], 0)
    return hpsi - project(inter, window)


def solution(mesh):
    sizes = {"zl": 2, "y": 8, "core": 2, "zh": 4, "x": 8}
    fine = Mesh(mesh.devices.reshape(tuple(sizes.values())), tuple(sizes))
    placed = P(BAND, GA)
    return jax.shard_map(
        on_device, mesh=fine, in_specs=(placed, placed), out_specs=placed, check_vma=False
    )
```

time: 221 us -> 81.7 us (0.37)
  the two profiles are of different devices: /device:TPU:128 before, /device:TPU:2 now
where the time goes in v1:
time: 81.7 us; the launch traced here: 81.3 us
  starting transfers between devices  36.9 us (45%)
  waiting for transfers between devices  35.7 us (44%)
  matrix products  6.5 us (8%)
  other arithmetic  1.16 us (1%)
  local copies, waits for them, and re-layouts  0.88 us (1%)
    ppermute x4, waiting for transfers between devices, shifted(): return lax.ppermute(value, BAND, pairs)  22.9 us
    all_to_all x1, starting transfers between devices, summed(): return jnp.sum(lax.all_to_all(copies, GA, 0, 0, tiled=True), 0)  20.5 us
    ppermute x4, starting transfers between devices, shifted(): return lax.ppermute(value, BAND, pairs)  14.6 us
    all_to_all x1, waiting for transfers between devices, summed(): return jnp.sum(lax.all_to_all(copies, GA, 0, 0, tiled=True), 0)  12.8 us
    dot_general x4, matrix products, overlap(): lax.dot_general(h, psi, (((1,), (1,)), ((), ())), precision=PRECISION, pr...  3.3 us
    dot_general x1, matrix products, project(): lax.dot_general(inter, psi, (((1,), (0,)), ((), ())), precision=PRECISION...  3.21 us
    ppermute x1, starting transfers between devices, swapped(): return lax.ppermute(value, 'core', [(0, 1), (1, 0)])  1.91 us
  transfers between devices with their start and end apart: 6, of which 5 were waited for; matrix products, arithmetic and copies ran while one was open for 5% of the time, Pallas kernels for 0%

profile of v1, /device:TPU:2, one launch (start us, length us, event | category | flops | bytes accessed | tf_op | source)
XLA Modules:
  0.0 81.3 jit_solution(8036153648049707311)
XLA Ops:
  0.0 8.3 %collective-permute-start.1 = (f32[32,6144]{1,0:T(8,128)}, f32[32,6144]{1,0:T(8,128)S(1)}, u32[]{:S(2)}, u32[]{:S(2)}) collective-permute-start(f32[32,6144]{1,0:T(8,128)} %param.3), channel_id=1, source_target_pairs={{0,992},{32,0},{64,32},{96,64},{128,96},{160,128},{192,160},{224,1... | collective-permute-start | bytes 2359304 | tf_op jit(solution)/shard_map/ppermute | solution.py:14
  8.3 1.9 %collective-permute-start = (f32[32,6144]{1,0:T(8,128)}, f32[32,6144]{1,0:T(8,128)S(1)}, u32[]{:S(2)}, u32[]{:S(2)}) collective-permute-start(f32[32,6144]{1,0:T(8,128)} %param.2), channel_id=1, source_target_pairs={{0,64},{32,96},{64,128},{96,160},{128,192},{160,224},{192,256},{22... | collective-permute-start | bytes 2359304 | tf_op jit(solution)/shard_map/ppermute | solution.py:14
  10.3 0.0 copy-start
  10.3 1.9 %fusion.8 = f32[32,32]{1,0:T(8,128)S(1)} fusion(f32[32,6144]{1,0:T(8,128)} %param.3, f32[32,6144]{1,0:T(8,128)} %param.2), kind=kOutput, calls=%fused_computation.12 | convolution fusion | flops 37748736 | bytes 1576960 | tf_op jit(solution)/shard_map/dot_general | solution.py:22
  12.2 6.0 %collective-permute-done.1 = f32[32,6144]{1,0:T(8,128)S(1)} collective-permute-done((f32[32,6144]{1,0:T(8,128)}, f32[32,6144]{1,0:T(8,128)S(1)}, u32[]{:S(2)}, u32[]{:S(2)}) %collective-permute-start.1) | collective-permute-done | bytes 786464 | tf_op jit(solution)/shard_map/ppermute | solution.py:14
  18.2 0.0 copy-done
  18.2 0.5 fusion.10
  18.7 0.0 copy-start.1
  18.7 10.5 %collective-permute-done = f32[32,6144]{1,0:T(8,128)S(1)} collective-permute-done((f32[32,6144]{1,0:T(8,128)}, f32[32,6144]{1,0:T(8,128)S(1)}, u32[]{:S(2)}, u32[]{:S(2)}) %collective-permute-start) | collective-permute-done | bytes 786464 | tf_op jit(solution)/shard_map/ppermute | solution.py:14
  29.2 0.5 fusion.11
  29.7 0.1 pad_maximum_fusion
  29.8 1.9 %collective-permute-start.2 = (f32[32,64]{1,0:T(8,128)S(1)}, f32[32,64]{1,0:T(8,128)S(1)}, u32[]{:S(2)}, u32[]{:S(2)}) collective-permute-start(f32[32,64]{1,0:T(8,128)S(1)} %pad_maximum_fusion), channel_id=1, source_target_pairs={{0,32},{32,64},{64,96},{96,128},{128,160},{160,192},{192,224},{224... | collective-permute-start | bytes 24584 | tf_op jit(solution)/shard_map/ppermute | solution.py:14
  31.7 0.5 fusion.9
  32.2 4.8 %collective-permute-done.2 = f32[32,64]{1,0:T(8,128)S(1)} collective-permute-done((f32[32,64]{1,0:T(8,128)S(1)}, f32[32,64]{1,0:T(8,128)S(1)}, u32[]{:S(2)}, u32[]{:S(2)}) %collective-permute-start.2) | collective-permute-done | bytes 8224 | tf_op jit(solution)/shard_map/ppermute | solution.py:14
  36.9 0.1 pad_maximum_fusion.1
  37.0 0.9 %broadcast_in_dim.2 = f32[32,32,128]{2,1,0:T(8,128)} broadcast(f32[32,128]{1,0:T(8,128)S(1)} %pad_maximum_fusion.1), dimensions={1,2} | broadcast | bytes 540672 | tf_op jit(solution)/shard_map/broadcast_in_dim | solution.py:35
  37.9 20.5 %all-to-all-start = ((f32[32,32,128]{2,1,0:T(8,128)}), f32[32,32,128]{2,1,0:T(8,128)S(1)}, u32[]{:S(2)}, u32[]{:S(2)}) async-start(f32[32,32,128]{2,1,0:T(8,128)} %broadcast_in_dim.2), calls=%async_computation | async-start | bytes 1048576 | tf_op jit(solution)/shard_map/all_to_all | solution.py:36
  58.4 1.0 %broadcast_select_fusion = f32[32,6144]{1,0:T(8,128)} fusion(f32[32,6144]{1,0:T(8,128)S(1)} %collective-permute-done, f32[32,6144]{1,0:T(8,128)S(1)} %copy-done, pred[]{:T(512)S(6)} %eq.3), kind=kLoop, calls=%fused_computation.8 | loop fusion | flops 196608 | bytes 2359297 | tf_op jit(solution)/shard_map/jit(_where)/select_n | solution.py:47
  59.3 1.9 %collective-permute-start.3 = (f32[32,6144]{1,0:T(8,128)}, f32[32,6144]{1,0:T(8,128)}, u32[]{:S(2)}, u32[]{:S(2)}) collective-permute-start(f32[32,6144]{1,0:T(8,128)} %broadcast_select_fusion), channel_id=1, source_target_pairs={{0,32},{32,0},{1,33},{33,1},{2,34},{34,2},{3,35},{35,3},{4,36},{36... | collective-permute-start | bytes 2359304 | tf_op jit(solution)/shard_map/ppermute | solution.py:18
  61.2 2.4 %collective-permute-start.4 = (f32[32,6144]{1,0:T(8,128)S(1)}, f32[32,6144]{1,0:T(8,128)}, u32[]{:S(2)}, u32[]{:S(2)}) collective-permute-start(f32[32,6144]{1,0:T(8,128)S(1)} %collective-permute-done), channel_id=1, source_target_pairs={{0,32},{32,64},{64,96},{96,128},{128,160},{160,192},{192,224},{224... | collective-permute-start | bytes 2359304 | tf_op jit(solution)/shard_map/ppermute | solution.py:14
  63.7 12.8 %all-to-all-done = f32[32,32,128]{2,1,0:T(8,128)S(1)} async-done(((f32[32,32,128]{2,1,0:T(8,128)}), f32[32,32,128]{2,1,0:T(8,128)S(1)}, u32[]{:S(2)}, u32[]{:S(2)}) %all-to-all-start) | async-done | bytes 524320 | tf_op jit(solution)/shard_map/all_to_all | solution.py:36
  76.5 0.0 collective-permute-done.3
  76.5 1.6 %collective-permute-done.4 = f32[32,6144]{1,0:T(8,128)} collective-permute-done((f32[32,6144]{1,0:T(8,128)S(1)}, f32[32,6144]{1,0:T(8,128)}, u32[]{:S(2)}, u32[]{:S(2)}) %collective-permute-start.4) | collective-permute-done | bytes 786464 | tf_op jit(solution)/shard_map/ppermute | solution.py:14
  78.1 3.2 %convolution_subtract_fusion = f32[32,6144]{1,0:T(8,128)} fusion(f32[32,6144]{1,0:T(8,128)S(1)} %copy-done.1, f32[32,128]{1,0:T(8,128)S(1)} %reduce_sum.9, f32[32,6144]{1,0:T(8,128)} %collective-permute-done.4, f32[32,6144]{1,0:T(8,128)} %collective-permute-done.3, f32[32,6144]{1,0:T(8,128)S(1)} %collective-permute-done, f32[32,6144]{1,0:T(8,128)S(1)} %copy-done), kind=kOutput, calls=%fused_computation | convolution fusion | flops 153550848 | bytes 4734976 | tf_op jit(solution)/shard_map/dot_general | solution.py:28
  (2 shorter events, 0.0 us)
Async XLA Ops:
  0.0 18.2 %collective-permute-start.1 = (f32[32,6144]{1,0:T(8,128)}, f32[32,6144]{1,0:T(8,128)S(1)}, u32[]{:S(2)}, u32[]{:S(2)}) collective-permute-start(f32[32,6144]{1,0:T(8,128)} %param.3), channel_id=1, source_target_pairs={{0,992},{32,0},{64,32},{96,64},{128,96},{160,128},{192,160},{224,1... | collective-permute-start | bytes 2359304 | tf_op jit(solution)/shard_map/ppermute | solution.py:14
  8.3 20.9 %collective-permute-start = (f32[32,6144]{1,0:T(8,128)}, f32[32,6144]{1,0:T(8,128)S(1)}, u32[]{:S(2)}, u32[]{:S(2)}) collective-permute-start(f32[32,6144]{1,0:T(8,128)} %param.2), channel_id=1, source_target_pairs={{0,64},{32,96},{64,128},{96,160},{128,192},{160,224},{192,256},{22... | collective-permute-start | bytes 2359304 | tf_op jit(solution)/shard_map/ppermute | solution.py:14
  10.3 7.9 %copy-start = (f32[32,6144]{1,0:T(8,128)S(1)}, f32[32,6144]{1,0:T(8,128)}, u32[]{:S(2)}) copy-start(f32[32,6144]{1,0:T(8,128)} %param.2) | copy-start | bytes 2359300
  18.7 13.0 %copy-start.1 = (f32[32,6144]{1,0:T(8,128)S(1)}, f32[32,6144]{1,0:T(8,128)}, u32[]{:S(2)}) copy-start(f32[32,6144]{1,0:T(8,128)} %param.3) | copy-start | bytes 2359300
  29.8 7.2 %collective-permute-start.2 = (f32[32,64]{1,0:T(8,128)S(1)}, f32[32,64]{1,0:T(8,128)S(1)}, u32[]{:S(2)}, u32[]{:S(2)}) collective-permute-start(f32[32,64]{1,0:T(8,128)S(1)} %pad_maximum_fusion), channel_id=1, source_target_pairs={{0,32},{32,64},{64,96},{96,128},{128,160},{160,192},{192,224},{224... | collective-permute-start | bytes 24584 | tf_op jit(solution)/shard_map/ppermute | solution.py:14
  37.9 38.6 %all-to-all-start = ((f32[32,32,128]{2,1,0:T(8,128)}), f32[32,32,128]{2,1,0:T(8,128)S(1)}, u32[]{:S(2)}, u32[]{:S(2)}) async-start(f32[32,32,128]{2,1,0:T(8,128)} %broadcast_in_dim.2), calls=%async_computation | async-start | bytes 1048576 | tf_op jit(solution)/shard_map/all_to_all | solution.py:36
  59.3 17.2 %collective-permute-start.3 = (f32[32,6144]{1,0:T(8,128)}, f32[32,6144]{1,0:T(8,128)}, u32[]{:S(2)}, u32[]{:S(2)}) collective-permute-start(f32[32,6144]{1,0:T(8,128)} %broadcast_select_fusion), channel_id=1, source_target_pairs={{0,32},{32,0},{1,33},{33,1},{2,34},{34,2},{3,35},{35,3},{4,36},{36... | collective-permute-start | bytes 2359304 | tf_op jit(solution)/shard_map/ppermute | solution.py:18
  61.2 16.9 %collective-permute-start.4 = (f32[32,6144]{1,0:T(8,128)S(1)}, f32[32,6144]{1,0:T(8,128)}, u32[]{:S(2)}, u32[]{:S(2)}) collective-permute-start(f32[32,6144]{1,0:T(8,128)S(1)} %collective-permute-done), channel_id=1, source_target_pairs={{0,32},{32,64},{64,96},{96,128},{128,160},{160,192},{192,224},{224... | collective-permute-start | bytes 2359304 | tf_op jit(solution)/shard_map/ppermute | solution.py:14

commit v2 on v1

v2 whole, which is shorter than its diff:
```python
import jax
import jax.numpy as jnp
from jax import lax
from jax.experimental import pallas as pl
from jax.experimental.pallas import tpu as pltpu
from jax.sharding import Mesh, PartitionSpec as P

BAND = ("zl", "y", "core")
GA = ("zh", "x")
PRECISION = lax.Precision.HIGH


def shifted(value, steps, start=0, stride=1):
    count = lax.axis_size(BAND)
    pairs = [(source, (source + steps) % count) for source in range(start, count, stride)]
    return lax.ppermute(value, BAND, pairs)


def overlap(h, psi):
    return lax.dot_general(
        h, psi, (((1,), (1,)), ((), ())), precision=PRECISION, preferred_element_type=jnp.float32
    )


def folded(left, right):
    return jnp.concatenate([left[:16], left[16:], right[:16], right[16:]], 1)


def spread(block, count):
    return jnp.broadcast_to(block[None], (count,) + block.shape)


def halves(value):
    high = value.astype(jnp.bfloat16)
    return high, (value - high.astype(jnp.float32)).astype(jnp.bfloat16)


def product(left, right, dims):
    rows = left.shape[0]
    left_high, left_low = halves(left)
    right_high, right_low = halves(right)
    one = lax.dot_general(
        jnp.concatenate([left_high, left_low], 0),
        right_high,
        (dims, ((), ())),
        preferred_element_type=jnp.float32,
    )
    two = lax.dot_general(left_high, right_low, (dims, ((), ())), preferred_element_type=jnp.float32)
    return one[:rows] + one[rows:] + two


SCALAR = pl.BlockSpec(memory_space=pltpu.SMEM)
VECTOR = pl.BlockSpec(memory_space=pltpu.VMEM)
PARAMS = pltpu.CompilerParams(vmem_limit_bytes=40 << 20)


def near(*arrays):
    return [pltpu.with_memory_space_constraint(x, pltpu.VMEM) for x in arrays]


def slots_kernel(
    odd_ref, h_ref, a_ref, psi_ref, odd2_ref, even2_ref, own_ref, ahead_ref, own_odd_ref, hop_ref,
    out_ref, beside_ref, behind2_ref
):
    half = out_ref.shape[0] // 2

    def put(start, left, right):
        block = folded(left, right)
        for k in range(half):
            out_ref[start + k] = block

    step = h_ref.shape[1] // 4

    @pl.when(odd_ref[0] == 0)
    def _():
        late = jnp.zeros((64, 32), jnp.float32)
        for k in range(4):
            at = pl.ds(k * step, step)
            late += product(
                jnp.concatenate([h_ref[:, at], a_ref[:, at]], 0), even2_ref[:, at], ((1,), (1,))
            )
            beside_ref[:, at] = psi_ref[:, at]
            behind2_ref[:, at] = even2_ref[:, at]
        put(0, own_ref[...], late[:32])
        put(half, ahead_ref[...], late[32:])

    @pl.when(odd_ref[0] == 1)
    def _():
        put(0, hop_ref[:, :32], hop_ref[:, 32:])
        put(half, own_ref[...], own_odd_ref[...])
        for k in range(4):
            at = pl.ds(k * step, step)
            beside_ref[:, at] = odd2_ref[:, at]
            behind2_ref[:, at] = odd2_ref[:, at]


def slots_of(odd, wide, small, count):
    shape = pltpu.VMEM(wide[0].shape, jnp.float32)
    return pl.pallas_call(
        slots_kernel,
        out_shape=[pltpu.VMEM((count, 16, 128), jnp.float32), shape, shape],
        in_specs=[SCALAR] + [VECTOR] * 9,
        out_specs=[VECTOR] * 3,
        compiler_params=PARAMS,
    )(odd, *near(*wide, *small))


def line_kernel(got_ref, out_ref):
    half = got_ref.shape[0] // 2
    line = jnp.concatenate([jnp.sum(got_ref[:half], 0), jnp.sum(got_ref[half:], 0)], 0)
    for k in range(out_ref.shape[0]):
        out_ref[k] = line


def line_of(got, count):
    return pl.pallas_call(
        line_kernel,
        out_shape=pltpu.VMEM((count, 32, 128), jnp.float32),
        in_specs=[VECTOR],
        out_specs=VECTOR,
        cost_estimate=pl.CostEstimate(flops=5_000_000_000, bytes_accessed=1024, transcendentals=0),
    )(*near(got))


def finish_kernel(
    odd_ref, got_ref, psi_ref, behind2_ref, behind3_ref, behind1_ref, h_ref,
    out_ref, h, made, into, out
):
    steps = into.shape[0]
    step = h.shape[1] // steps
    loads = []
    for k in range(steps):
        at = pl.ds(k * step, step)
        loads.append(pltpu.make_async_copy(h_ref.at[:, at], h.at[:, at], into.at[k]))
        loads[-1].start()

    total = jnp.sum(got_ref[...], 0)
    odd = odd_ref[0] == 1
    own = jnp.where(odd, total[16:], total[:16])
    ahead = jnp.where(odd, total[:16], total[16:])

    def unfolded(block):
        return [
            jnp.concatenate([block[:, k : k + 32], block[:, k + 32 : k + 64]], 0) for k in (0, 64)
        ]

    mine, next_to = unfolded(own), unfolded(ahead)
    high, low = halves(jnp.concatenate(mine + next_to[::-1], 1))
    both = jnp.concatenate([high, low], 0)

    def times(left, right):
        return lax.dot_general(
            left, right, (((1,), (0,)), ((), ())), preferred_element_type=jnp.float32
        )

    stores = []
    for k in range(steps):
        at = pl.ds(k * step, step)
        blocks = [ref[:, at] for ref in (psi_ref, behind2_ref, behind3_ref, behind1_ref)]
        window_high, window_low = halves(jnp.concatenate(blocks, 0))
        one, two = times(both, window_high), times(high, window_low)
        loads[k].wait()
        made[:, at] = h[:, at] - (one[:32] + one[32:] + two)
        stores.append(pltpu.make_async_copy(made.at[:, at], out_ref.at[:, at], out.at[k]))
        stores[-1].start()
    for copy in stores:
        copy.wait()


def finished(odd, got, window, hpsi):
    block = pltpu.VMEM(hpsi.shape, jnp.float32)
    return pl.pallas_call(
        finish_kernel,
        out_shape=jax.ShapeDtypeStruct(hpsi.shape, jnp.float32),
        in_specs=[SCALAR] + [VECTOR] * 5 + [pl.BlockSpec(memory_space=pl.ANY)],
        out_specs=pl.BlockSpec(memory_space=pl.ANY),
        scratch_shapes=[block, block, pltpu.SemaphoreType.DMA((6,)), pltpu.SemaphoreType.DMA((6,))],
        compiler_params=PARAMS,
    )(odd, *near(got, *window), hpsi)


def on_device(psi, hpsi):
    core = lax.axis_index("core")
    odd = core.astype(jnp.int32).reshape(1)
    odd2 = shifted(psi, 2, 1, 2)
    ahead1 = shifted(hpsi, -1)
    own, own_odd = overlap(hpsi, psi), overlap(hpsi, odd2)
    psi_later, own, own_odd = lax.optimization_barrier((psi, own, own_odd))
    even2 = shifted(psi_later, 2, 0, 2)

    ahead, ahead_odd = overlap(ahead1, psi), overlap(ahead1, odd2)
    hopped = shifted(jnp.concatenate([ahead, ahead_odd], 1), 2, 1, 2)

    slots, beside, behind2 = slots_of(
        odd,
        (hpsi, ahead1, psi, odd2, even2),
        (own, ahead, own_odd, hopped),
        2 * lax.axis_size("x"),
    )
    got = lax.all_to_all(slots, ("core", "x"), 0, 0, tiled=True)
    line = line_of(got, lax.axis_size("zh"))
    behind3 = shifted(behind2, 1)
    behind1 = lax.ppermute(beside, "core", [(0, 1), (1, 0)])
    got = lax.all_to_all(line, "zh", 0, 0, tiled=True)
    return finished(odd, got, (psi, behind2, behind3, behind1), hpsi)


def solution(mesh):
    sizes = {"zl": 2, "y": 8, "core": 2, "zh": 4, "x": 8}
    fine = Mesh(mesh.devices.reshape(tuple(sizes.values())), tuple(sizes))
    placed = P(BAND, GA)
    return jax.shard_map(
        on_device, mesh=fine, in_specs=(placed, placed), out_specs=placed, check_vma=False
    )
```

time: 81.7 us -> 76.7 us (0.939)
  the two profiles are of different devices: /device:TPU:2 before, /device:TPU:1 now
where the time goes in v2:
time: 76.7 us; the launch traced here: 76.2 us
  starting transfers between devices  29.8 us (39%)
  blocking collectives  21.3 us (28%)
  waiting for transfers between devices  14.1 us (18%)
  Pallas kernels  5.53 us (7%)
  matrix products  3.22 us (4%)
  local copies, waits for them, and re-layouts  2.07 us (3%)
    ppermute x5, starting transfers between devices, shifted(): return lax.ppermute(value, BAND, pairs)  22.4 us
    all_to_all x1, blocking collectives, on_device(): got = lax.all_to_all(line, 'zh', 0, 0, tiled=True)  21.3 us
    ppermute x5, waiting for transfers between devices, shifted(): return lax.ppermute(value, BAND, pairs)  10.9 us
    all_to_all x1, starting transfers between devices, on_device(): got = lax.all_to_all(slots, ('core', 'x'), 0, 0, tiled=True)  5.31 us
    pallas_call x1, Pallas kernels, finished(): pl.pallas_call(finish_kernel, out_shape=jax.ShapeDtypeStruct(hpsi.shape,...  3.62 us
    dot_general x4, matrix products, overlap(): lax.dot_general(h, psi, (((1,), (1,)), ((), ())), precision=PRECISION, pr...  3.22 us
    all_to_all x1, waiting for transfers between devices, on_device(): got = lax.all_to_all(slots, ('core', 'x'), 0, 0, tiled=True)  3.2 us
    ppermute x1, starting transfers between devices, on_device(): behind1 = lax.ppermute(beside, 'core', [(0, 1), (1, 0)])  2.08 us
  transfers between devices with their start and end apart: 7, of which 3 were waited for; matrix products, arithmetic and copies ran while one was open for 4% of the time, Pallas kernels for 0%

profile of v2, /device:TPU:1, one launch (start us, length us, event | category | flops | bytes accessed | tf_op | source)
XLA Modules:
  0.0 76.2 jit_solution(17461425453077851837)
XLA Ops:
  0.0 4.3 %collective-permute-start.1 = (f32[32,6144]{1,0:T(8,128)}, f32[32,6144]{1,0:T(8,128)S(1)}, u32[]{:S(2)}, u32[]{:S(2)}) collective-permute-start(f32[32,6144]{1,0:T(8,128)} %psi_ref.3), channel_id=1, source_target_pairs={{32,96},{96,160},{160,224},{224,288},{288,352},{352,416},{416,480}... | collective-permute-start | bytes 2359304 | tf_op jit(solution)/shard_map/ppermute | solution.py:16
  4.3 12.6 %collective-permute-start = (f32[32,6144]{1,0:T(8,128)}, f32[32,6144]{1,0:T(8,128)S(1)}, u32[]{:S(2)}, u32[]{:S(2)}) collective-permute-start(f32[32,6144]{1,0:T(8,128)} %h_ref.3), channel_id=1, source_target_pairs={{0,992},{32,0},{64,32},{96,64},{128,96},{160,128},{192,160},{224,1... | collective-permute-start | bytes 2359304 | tf_op jit(solution)/shard_map/ppermute | solution.py:16
  16.9 1.8 %fusion.own_ref = f32[32,32]{1,0:T(8,128)S(1)} fusion(f32[32,6144]{1,0:T(8,128)} %h_ref.3, f32[32,6144]{1,0:T(8,128)} %psi_ref.3), kind=kOutput, calls=%fused_computation.1 | convolution fusion | flops 37748736 | bytes 1576960 | tf_op jit(solution)/shard_map/dot_general | solution.py:20
  18.7 0.0 copy-start.1
  18.8 0.4 collective-permute-done.1.odd2_ref
  19.2 0.5 fusion.1.own_odd_ref
  19.6 0.3 copy-done.1
  19.9 1.6 %collective-permute-start.2 = (f32[32,6144]{1,0:T(8,128)S(1)}, f32[32,6144]{1,0:T(8,128)}, u32[]{:S(2)}, u32[]{:S(2)}) collective-permute-start(f32[32,6144]{1,0:T(8,128)S(1)} %copy-done.1), channel_id=1, source_target_pairs={{0,64},{64,128},{128,192},{192,256},{256,320},{320,384},{384,448},... | collective-permute-start | bytes 2359304 | tf_op jit(solution)/shard_map/ppermute | solution.py:16
  21.4 0.5 fusion.2.ahead_ref
  21.9 0.5 fusion.3
  22.4 0.1 pad_maximum_fusion
  22.5 1.9 %collective-permute-start.3 = (f32[32,64]{1,0:T(8,128)S(1)}, f32[32,64]{1,0:T(8,128)S(1)}, u32[]{:S(2)}, u32[]{:S(2)}) collective-permute-start(f32[32,64]{1,0:T(8,128)S(1)} %pad_maximum_fusion), channel_id=1, source_target_pairs={{32,96},{96,160},{160,224},{224,288},{288,352},{352,416},{416,480}... | collective-permute-start | bytes 24584 | tf_op jit(solution)/shard_map/ppermute | solution.py:16
  24.4 10.5 %collective-permute-done.3.hop_ref = f32[32,64]{1,0:T(8,128)S(1)} collective-permute-done((f32[32,64]{1,0:T(8,128)S(1)}, f32[32,64]{1,0:T(8,128)S(1)}, u32[]{:S(2)}, u32[]{:S(2)}) %collective-permute-start.3) | collective-permute-done | bytes 8224 | tf_op jit(solution)/shard_map/ppermute | solution.py:16
  34.9 0.0 collective-permute-done.2.even2_ref
  34.9 1.9 %shard_map.28 = (f32[16,16,128]{2,1,0:T(8,128)}, f32[32,6144]{1,0:T(8,128)S(1)}, f32[32,6144]{1,0:T(8,128)S(1)}) custom-call(s32[1]{0:T(128)} %bitcast.odd_ref, f32[32,6144]{1,0:T(8,128)S(1)} %copy-done, f32[32,6144]{1,0:T(8,128)S(1)} %collective-permute-done.a_ref, f32[32,6144]{1,0:T(8,128)S(1)} %copy-done.1, ...), custom_call_target="tpu_custom_call" | custom-call | tf_op jit(solution)/shard_map/pallas_call | solution.py:99
  36.8 0.9 %copy-done.2 = f32[32,6144]{1,0:T(8,128)} copy-done((f32[32,6144]{1,0:T(8,128)}, f32[32,6144]{1,0:T(8,128)S(1)}, u32[]{:S(2)}) %copy-start.2) | copy-done | bytes 786456
  37.7 0.9 %copy-done.4 = f32[32,6144]{1,0:T(8,128)} copy-done((f32[32,6144]{1,0:T(8,128)}, f32[32,6144]{1,0:T(8,128)S(1)}, u32[]{:S(2)}) %copy-start.4) | copy-done | bytes 786456
  38.6 5.3 %all-to-all-start = ((f32[16,16,128]{2,1,0:T(8,128)}), f32[16,16,128]{2,1,0:T(8,128)S(1)}, u32[]{:S(2)}, u32[]{:S(2)}) async-start(f32[16,16,128]{2,1,0:T(8,128)} %get-tuple-element.14), calls=%async_computation | async-start | bytes 262144 | tf_op jit(solution)/shard_map/all_to_all | solution.py:200
  43.9 2.1 %collective-permute-start.5 = (f32[32,6144]{1,0:T(8,128)}, f32[32,6144]{1,0:T(8,128)S(1)}, u32[]{:S(2)}, u32[]{:S(2)}) collective-permute-start(f32[32,6144]{1,0:T(8,128)} %copy-done.4), channel_id=1, source_target_pairs={{0,32},{32,0},{1,33},{33,1},{2,34},{34,2},{3,35},{35,3},{4,36},{36... | collective-permute-start | bytes 2359304 | tf_op jit(solution)/shard_map/ppermute | solution.py:203
  46.0 0.0 copy-start.3
  46.0 2.1 %collective-permute-start.4 = (f32[32,6144]{1,0:T(8,128)}, f32[32,6144]{1,0:T(8,128)}, u32[]{:S(2)}, u32[]{:S(2)}) collective-permute-start(f32[32,6144]{1,0:T(8,128)} %copy-done.2), channel_id=1, source_target_pairs={{0,32},{32,64},{64,96},{96,128},{128,160},{160,192},{192,224},{224... | collective-permute-start | bytes 2359304 | tf_op jit(solution)/shard_map/ppermute | solution.py:16
  48.1 3.2 %all-to-all-done.got_ref = f32[16,16,128]{2,1,0:T(8,128)S(1)} async-done(((f32[16,16,128]{2,1,0:T(8,128)}), f32[16,16,128]{2,1,0:T(8,128)S(1)}, u32[]{:S(2)}, u32[]{:S(2)}) %all-to-all-start) | async-done | bytes 131104 | tf_op jit(solution)/shard_map/all_to_all | solution.py:200
  51.3 21.3 %all_to_all.10.got_ref = f32[4,32,128]{2,1,0:T(8,128)S(1)} all-to-all(f32[4,32,128]{2,1,0:T(8,128)S(1)} %shard_map.29), channel_id=1, replica_groups=mesh['zl'=2,'y'=8,'core'=2,'zh'=4,'x'=8] {'zh'}, dimensions={0} | all-to-all | bytes 131072 | tf_op jit(solution)/shard_map/all_to_all | solution.py:204
  72.6 3.6 %shard_map.30 = f32[32,6144]{1,0:T(8,128)} custom-call(s32[1]{0:T(128)} %bitcast.odd_ref, f32[4,32,128]{2,1,0:T(8,128)S(1)} %all_to_all.10.got_ref, f32[32,6144]{1,0:T(8,128)S(1)} %copy-done.1, f32[32,6144]{1,0:T(8,128)S(1)} %copy-done.3, f32[32,6144]{1,0:T(8,128)} %collective-permute-done.4.behind3_ref, f32[32,6144]{1,0:T(8,128)S(1)} %collective-permute-done.5.behind1_ref, ...), custom_call_target="tpu_custom_call" | custom-call | tf_op jit(solution)/shard_map/pallas_call | solution.py:172
  (9 shorter events, 0.0 us)
Async XLA Ops:
  0.0 19.1 %copy-start = (f32[32,6144]{1,0:T(8,128)S(1)}, f32[32,6144]{1,0:T(8,128)}, u32[]{:S(2)}) copy-start(f32[32,6144]{1,0:T(8,128)} %h_ref.3) | copy-start | bytes 2359300
  0.0 19.1 %collective-permute-start.1 = (f32[32,6144]{1,0:T(8,128)}, f32[32,6144]{1,0:T(8,128)S(1)}, u32[]{:S(2)}, u32[]{:S(2)}) collective-permute-start(f32[32,6144]{1,0:T(8,128)} %psi_ref.3), channel_id=1, source_target_pairs={{32,96},{96,160},{160,224},{224,288},{288,352},{352,416},{416,480}... | collective-permute-start | bytes 2359304 | tf_op jit(solution)/shard_map/ppermute | solution.py:16
  4.3 17.2 %collective-permute-start = (f32[32,6144]{1,0:T(8,128)}, f32[32,6144]{1,0:T(8,128)S(1)}, u32[]{:S(2)}, u32[]{:S(2)}) collective-permute-start(f32[32,6144]{1,0:T(8,128)} %h_ref.3), channel_id=1, source_target_pairs={{0,992},{32,0},{64,32},{96,64},{128,96},{160,128},{192,160},{224,1... | collective-permute-start | bytes 2359304 | tf_op jit(solution)/shard_map/ppermute | solution.py:16
  18.7 1.1 %copy-start.1 = (f32[32,6144]{1,0:T(8,128)S(1)}, f32[32,6144]{1,0:T(8,128)}, u32[]{:S(2)}) copy-start(f32[32,6144]{1,0:T(8,128)} %psi_ref.3) | copy-start | bytes 2359300
  19.9 15.0 %collective-permute-start.2 = (f32[32,6144]{1,0:T(8,128)S(1)}, f32[32,6144]{1,0:T(8,128)}, u32[]{:S(2)}, u32[]{:S(2)}) collective-permute-start(f32[32,6144]{1,0:T(8,128)S(1)} %copy-done.1), channel_id=1, source_target_pairs={{0,64},{64,128},{128,192},{192,256},{256,320},{320,384},{384,448},... | collective-permute-start | bytes 2359304 | tf_op jit(solution)/shard_map/ppermute | solution.py:16
  22.5 12.5 %collective-permute-start.3 = (f32[32,64]{1,0:T(8,128)S(1)}, f32[32,64]{1,0:T(8,128)S(1)}, u32[]{:S(2)}, u32[]{:S(2)}) collective-permute-start(f32[32,64]{1,0:T(8,128)S(1)} %pad_maximum_fusion), channel_id=1, source_target_pairs={{32,96},{96,160},{160,224},{224,288},{288,352},{352,416},{416,480}... | collective-permute-start | bytes 24584 | tf_op jit(solution)/shard_map/ppermute | solution.py:16
  36.8 0.9 %copy-start.2 = (f32[32,6144]{1,0:T(8,128)}, f32[32,6144]{1,0:T(8,128)S(1)}, u32[]{:S(2)}) copy-start(f32[32,6144]{1,0:T(8,128)S(1)} %get-tuple-element.15.behind2_ref) | copy-start | bytes 2359300
  37.7 0.9 %copy-start.4 = (f32[32,6144]{1,0:T(8,128)}, f32[32,6144]{1,0:T(8,128)S(1)}, u32[]{:S(2)}) copy-start(f32[32,6144]{1,0:T(8,128)S(1)} %get-tuple-element.16) | copy-start | bytes 2359300
  38.6 12.7 %all-to-all-start = ((f32[16,16,128]{2,1,0:T(8,128)}), f32[16,16,128]{2,1,0:T(8,128)S(1)}, u32[]{:S(2)}, u32[]{:S(2)}) async-start(f32[16,16,128]{2,1,0:T(8,128)} %get-tuple-element.14), calls=%async_computation | async-start | bytes 262144 | tf_op jit(solution)/shard_map/all_to_all | solution.py:200
  43.9 28.7 %collective-permute-start.5 = (f32[32,6144]{1,0:T(8,128)}, f32[32,6144]{1,0:T(8,128)S(1)}, u32[]{:S(2)}, u32[]{:S(2)}) collective-permute-start(f32[32,6144]{1,0:T(8,128)} %copy-done.4), channel_id=1, source_target_pairs={{0,32},{32,0},{1,33},{33,1},{2,34},{34,2},{3,35},{35,3},{4,36},{36... | collective-permute-start | bytes 2359304 | tf_op jit(solution)/shard_map/ppermute | solution.py:203
  46.0 26.6 %copy-start.3 = (f32[32,6144]{1,0:T(8,128)S(1)}, f32[32,6144]{1,0:T(8,128)}, u32[]{:S(2)}) copy-start(f32[32,6144]{1,0:T(8,128)} %copy-done.2) | copy-start | bytes 2359300
  46.0 26.6 %collective-permute-start.4 = (f32[32,6144]{1,0:T(8,128)}, f32[32,6144]{1,0:T(8,128)}, u32[]{:S(2)}, u32[]{:S(2)}) collective-permute-start(f32[32,6144]{1,0:T(8,128)} %copy-done.2), channel_id=1, source_target_pairs={{0,32},{32,64},{64,96},{96,128},{128,160},{160,192},{192,224},{224... | collective-permute-start | bytes 2359304 | tf_op jit(solution)/shard_map/ppermute | solution.py:16

commit v3 on v2

v3 whole, which is shorter than its diff:
```python
import jax
import jax.numpy as jnp
from jax import lax
from jax.experimental import pallas as pl
from jax.experimental.pallas import tpu as pltpu
from jax.sharding import Mesh, PartitionSpec as P

BAND = ("zl", "y", "core")
GA = ("zh", "x")
PRECISION = lax.Precision.HIGH


def shifted(value, steps, start=0, stride=1):
    count = lax.axis_size(BAND)
    pairs = [(source, (source + steps) % count) for source in range(start, count, stride)]
    return lax.ppermute(value, BAND, pairs)


def overlap(h, psi):
    return lax.dot_general(
        h, psi, (((1,), (1,)), ((), ())), precision=PRECISION, preferred_element_type=jnp.float32
    )


def folded(left, right):
    return jnp.concatenate([left[:16], left[16:], right[:16], right[16:]], 1)


def spread(block, count):
    return jnp.broadcast_to(block[None], (count,) + block.shape)


def halves(value):
    high = value.astype(jnp.bfloat16)
    return high, (value - high.astype(jnp.float32)).astype(jnp.bfloat16)


def product(left, right, dims):
    rows = left.shape[0]
    left_high, left_low = halves(left)
    right_high, right_low = halves(right)
    one = lax.dot_general(
        jnp.concatenate([left_high, left_low], 0),
        right_high,
        (dims, ((), ())),
        preferred_element_type=jnp.float32,
    )
    two = lax.dot_general(left_high, right_low, (dims, ((), ())), preferred_element_type=jnp.float32)
    return one[:rows] + one[rows:] + two


SCALAR = pl.BlockSpec(memory_space=pltpu.SMEM)
VECTOR = pl.BlockSpec(memory_space=pltpu.VMEM)
PARAMS = pltpu.CompilerParams(vmem_limit_bytes=40 << 20)


def near(*arrays):
    return [pltpu.with_memory_space_constraint(x, pltpu.VMEM) for x in arrays]


def slots_kernel(odd_ref, h_ref, a_ref, even_ref, own_ref, ahead_ref, own_odd_ref, hop_ref, out_ref):
    half = out_ref.shape[0] // 2

    def put(start, left, right):
        block = folded(left, right)
        for k in range(half):
            out_ref[start + k] = block

    @pl.when(odd_ref[0] == 0)
    def _():
        step = h_ref.shape[1] // 4
        late = jnp.zeros((64, 32), jnp.float32)
        for k in range(4):
            at = pl.ds(k * step, step)
            late += product(
                jnp.concatenate([h_ref[:, at], a_ref[:, at]], 0), even_ref[:, at], ((1,), (1,))
            )
        put(0, own_ref[...], late[:32])
        put(half, ahead_ref[...], late[32:])

    @pl.when(odd_ref[0] == 1)
    def _():
        put(0, hop_ref[:, :32], hop_ref[:, 32:])
        put(half, own_ref[...], own_odd_ref[...])


def slots_of(odd, wide, small, count):
    return pl.pallas_call(
        slots_kernel,
        out_shape=jax.ShapeDtypeStruct((count, 16, 128), jnp.float32),
        in_specs=[SCALAR] + [VECTOR] * 7,
        out_specs=VECTOR,
        compiler_params=PARAMS,
    )(odd, *near(*wide), *small)


def line_kernel(got_ref, out_ref):
    half = got_ref.shape[0] // 2
    line = jnp.concatenate([jnp.sum(got_ref[:half], 0), jnp.sum(got_ref[half:], 0)], 0)
    for k in range(out_ref.shape[0]):
        out_ref[k] = line


def line_of(got, count):
    return pl.pallas_call(
        line_kernel,
        out_shape=pltpu.VMEM((count, 32, 128), jnp.float32),
        in_specs=[VECTOR],
        out_specs=VECTOR,
        cost_estimate=pl.CostEstimate(flops=5_000_000_000, bytes_accessed=1024, transcendentals=0),
    )(*near(got))


def total_kernel(odd_ref, got_ref, out_ref):
    total = jnp.sum(got_ref[...], 0)
    odd = odd_ref[0] == 1
    own = jnp.where(odd, total[16:], total[:16])
    ahead = jnp.where(odd, total[:16], total[16:])
    for n, block in enumerate((own, ahead)):
        for k in range(2):
            rows = [block[:, 64 * k + 32 * r : 64 * k + 32 * r + 32] for r in range(2)]
            out_ref[:, 64 * n + 32 * k : 64 * n + 32 * k + 32] = jnp.concatenate(rows, 0)


def total_of(odd, got):
    return pl.pallas_call(
        total_kernel,
        out_shape=pltpu.VMEM((32, 128), jnp.float32),
        in_specs=[SCALAR, VECTOR],
        out_specs=VECTOR,
        cost_estimate=pl.CostEstimate(
            flops=5_000_000_000, bytes_accessed=1024, transcendentals=0
        ),
    )(odd, *near(got))


def finish_kernel(
    odd_ref, inter_ref, psi_ref, odd1_ref, even1_ref, odd2_ref, even2_ref, odd3_ref, even3_ref, h_ref,
    out_ref, h, made, into, out
):
    steps = into.shape[0]
    step = h.shape[1] // steps
    loads = []
    for k in range(steps):
        at = pl.ds(k * step, step)
        loads.append(pltpu.make_async_copy(h_ref.at[:, at], h.at[:, at], into.at[k]))
        loads[-1].start()
    inter = inter_ref[...]

    def finish(*behind):
        stores = []
        for k in range(steps):
            at = pl.ds(k * step, step)
            window = jnp.concatenate([ref[:, at] for ref in (psi_ref,) + behind], 0)
            shift = product(inter, window, ((1,), (0,)))
            loads[k].wait()
            made[:, at] = h[:, at] - shift
            stores.append(pltpu.make_async_copy(made.at[:, at], out_ref.at[:, at], out.at[k]))
            stores[-1].start()
        for copy in stores:
            copy.wait()

    @pl.when(odd_ref[0] == 0)
    def _():
        finish(even2_ref, odd1_ref, odd3_ref)

    @pl.when(odd_ref[0] == 1)
    def _():
        finish(odd2_ref, even1_ref, even3_ref)


def finished(odd, inter, blocks, hpsi):
    block = pltpu.VMEM(hpsi.shape, jnp.float32)
    return pl.pallas_call(
        finish_kernel,
        out_shape=jax.ShapeDtypeStruct(hpsi.shape, jnp.float32),
        in_specs=[SCALAR] + [VECTOR] * 8 + [pl.BlockSpec(memory_space=pl.ANY)],
        out_specs=pl.BlockSpec(memory_space=pl.ANY),
        scratch_shapes=[block, block, pltpu.SemaphoreType.DMA((6,)), pltpu.SemaphoreType.DMA((6,))],
        compiler_params=PARAMS,
    )(odd, *near(inter, *blocks), hpsi)


def on_device(psi, hpsi):
    odd = lax.axis_index("core").astype(jnp.int32).reshape(1)
    odd2 = shifted(psi, 2, 1, 2)
    ahead1 = shifted(hpsi, -1)
    own, own_odd = overlap(hpsi, psi), overlap(hpsi, odd2)
    psi_later, own, own_odd = lax.optimization_barrier((psi, own, own_odd))
    even2 = shifted(psi_later, 2, 0, 2)

    ahead, ahead_odd = overlap(ahead1, psi), overlap(ahead1, odd2)
    hopped = shifted(jnp.concatenate([ahead, ahead_odd], 1), 2, 1, 2)
    even1 = lax.ppermute(psi, "core", [(0, 1)])

    slots = slots_of(
        odd, (hpsi, ahead1, even2), (own, ahead, own_odd, hopped), 2 * lax.axis_size("x")
    )
    slots, odd2_later = lax.optimization_barrier((slots, odd2))
    got = lax.all_to_all(slots, ("core", "x"), 0, 0, tiled=True)
    odd3 = shifted(odd2_later, 1, 1, 2)
    line = line_of(got, lax.axis_size("zh"))
    line, odd2_last, even2_last = lax.optimization_barrier((line, odd2, even2))
    got = lax.all_to_all(line, "zh", 0, 0, tiled=True)
    odd1 = lax.ppermute(odd2_last, "core", [(1, 0)])
    even3 = lax.ppermute(even2_last, "core", [(0, 1)])
    inter = total_of(odd, got)
    return finished(odd, inter, (psi, odd1, even1, odd2, even2, odd3, even3), hpsi)


def solution(mesh):
    sizes = {"zl": 2, "y": 8, "core": 2, "zh": 4, "x": 8}
    fine = Mesh(mesh.devices.reshape(tuple(sizes.values())), tuple(sizes))
    placed = P(BAND, GA)
    return jax.shard_map(
        on_device, mesh=fine, in_specs=(placed, placed), out_specs=placed, check_vma=False
    )
```

time: 76.7 us -> 81.7 us (1.065)
  the two profiles are of different devices: /device:TPU:1 before, /device:TPU:2 now
where the time goes in v3:
time: 81.7 us; the launch traced here: 81.2 us
  starting transfers between devices  31.3 us (38%)
  blocking collectives  21.3 us (26%)
  waiting for transfers between devices  17.5 us (21%)
  Pallas kernels  7 us (9%)
  matrix products  3.22 us (4%)
    all_to_all x1, blocking collectives, on_device(): got = lax.all_to_all(line, 'zh', 0, 0, tiled=True)  21.3 us
    ppermute x5, starting transfers between devices, shifted(): return lax.ppermute(value, BAND, pairs)  14.2 us
    ppermute x5, waiting for transfers between devices, shifted(): return lax.ppermute(value, BAND, pairs)  12.7 us
    all_to_all x1, starting transfers between devices, on_device(): got = lax.all_to_all(slots, ('core', 'x'), 0, 0, tiled=True)  8.86 us
    all_to_all x1, waiting for transfers between devices, on_device(): got = lax.all_to_all(slots, ('core', 'x'), 0, 0, tiled=True)  4.84 us
    ppermute x1, starting transfers between devices, on_device(): even3 = lax.ppermute(even2_last, 'core', [(0, 1)])  4.82 us
    pallas_call x1, Pallas kernels, finished(): pl.pallas_call(finish_kernel, out_shape=jax.ShapeDtypeStruct(hpsi.shape,...  4.22 us
    dot_general x4, matrix products, overlap(): lax.dot_general(h, psi, (((1,), (1,)), ((), ())), precision=PRECISION, pr...  3.22 us
  transfers between devices with their start and end apart: 9, of which 3 were waited for; matrix products, arithmetic and copies ran while one was open for 4% of the time, Pallas kernels for 0%

profile of v3, /device:TPU:2, one launch (start us, length us, event | category | flops | bytes accessed | tf_op | source)
XLA Modules:
  0.0 81.2 jit_solution(6854486229592813033)
XLA Ops:
  0.0 0.8 %collective-permute-start.1 = (f32[32,6144]{1,0:T(8,128)}, f32[32,6144]{1,0:T(8,128)S(1)}, u32[]{:S(2)}, u32[]{:S(2)}) collective-permute-start(f32[32,6144]{1,0:T(8,128)} %psi_ref.1), channel_id=1, source_target_pairs={{32,96},{96,160},{160,224},{224,288},{288,352},{352,416},{416,480}... | collective-permute-start | bytes 2359304 | tf_op jit(solution)/shard_map/ppermute | solution.py:16
  0.8 9.5 %collective-permute-start = (f32[32,6144]{1,0:T(8,128)}, f32[32,6144]{1,0:T(8,128)S(1)}, u32[]{:S(2)}, u32[]{:S(2)}) collective-permute-start(f32[32,6144]{1,0:T(8,128)} %h_ref.3), channel_id=1, source_target_pairs={{0,992},{32,0},{64,32},{96,64},{128,96},{160,128},{192,160},{224,1... | collective-permute-start | bytes 2359304 | tf_op jit(solution)/shard_map/ppermute | solution.py:16
  10.4 1.8 %fusion.own_ref = f32[32,32]{1,0:T(8,128)S(1)} fusion(f32[32,6144]{1,0:T(8,128)} %h_ref.3, f32[32,6144]{1,0:T(8,128)} %psi_ref.1), kind=kOutput, calls=%fused_computation.1 | convolution fusion | flops 37748736 | bytes 1576960 | tf_op jit(solution)/shard_map/dot_general | solution.py:20
  12.2 0.0 copy-start.1
  12.3 0.5 fusion.1.own_odd_ref
  12.7 0.6 copy-done.1
  13.4 1.9 %collective-permute-start.2 = (f32[32,6144]{1,0:T(8,128)S(1)}, f32[32,6144]{1,0:T(8,128)}, u32[]{:S(2)}, u32[]{:S(2)}) collective-permute-start(f32[32,6144]{1,0:T(8,128)S(1)} %copy-done.1), channel_id=1, source_target_pairs={{0,64},{64,128},{128,192},{192,256},{256,320},{320,384},{384,448},... | collective-permute-start | bytes 2359304 | tf_op jit(solution)/shard_map/ppermute | solution.py:16
  15.3 4.9 %collective-permute-done.a_ref = f32[32,6144]{1,0:T(8,128)S(1)} collective-permute-done((f32[32,6144]{1,0:T(8,128)}, f32[32,6144]{1,0:T(8,128)S(1)}, u32[]{:S(2)}, u32[]{:S(2)}) %collective-permute-start) | collective-permute-done | bytes 786464 | tf_op jit(solution)/shard_map/ppermute | solution.py:16
  20.2 0.5 fusion.2.ahead_ref
  20.7 0.5 fusion.3
  21.2 0.1 pad_maximum_fusion
  21.2 0.7 collective-permute-start.3
  21.9 7.7 %collective-permute-done.2.even_ref.even2_ref = f32[32,6144]{1,0:T(8,128)} collective-permute-done((f32[32,6144]{1,0:T(8,128)S(1)}, f32[32,6144]{1,0:T(8,128)}, u32[]{:S(2)}, u32[]{:S(2)}) %collective-permute-start.2) | collective-permute-done | bytes 786464 | tf_op jit(solution)/shard_map/ppermute | solution.py:16
  29.6 2.6 %shard_map.28 = f32[16,16,128]{2,1,0:T(8,128)} custom-call(s32[1]{0:T(128)} %bitcast.odd_ref, f32[32,6144]{1,0:T(8,128)S(1)} %copy-done, f32[32,6144]{1,0:T(8,128)S(1)} %collective-permute-done.a_ref, f32[32,6144]{1,0:T(8,128)} %collective-permute-done.2.even_ref.even2_ref, f32[32,32]{1,0:T(8,128)S(1)} %fusion.own_ref, f32[32,32]{1,0:T(8,128)S(1)} %fusion.2.ahead_ref, ...), custom_call_target="tpu_custom_call" | custom-call | tf_op jit(solution)/shard_map/pallas_call | solution.py:88
  32.3 8.9 %all-to-all-start = ((f32[16,16,128]{2,1,0:T(8,128)}), f32[16,16,128]{2,1,0:T(8,128)S(1)}, u32[]{:S(2)}, u32[]{:S(2)}) async-start(f32[16,16,128]{2,1,0:T(8,128)} %shard_map.28), calls=%async_computation | async-start | bytes 262144 | tf_op jit(solution)/shard_map/all_to_all | solution.py:200
  41.1 2.1 %collective-permute-start.5 = (f32[32,6144]{1,0:T(8,128)S(1)}, f32[32,6144]{1,0:T(8,128)S(1)}, u32[]{:S(2)}, u32[]{:S(2)}) collective-permute-start(f32[32,6144]{1,0:T(8,128)S(1)} %copy-done.1), channel_id=1, source_target_pairs={{0,32},{1,33},{2,34},{3,35},{4,36},{5,37},{6,38},{7,39},{8,40},{9,... | collective-permute-start | bytes 2359304 | tf_op jit(solution)/shard_map/ppermute | solution.py:194
  43.2 1.3 %collective-permute-start.6 = (f32[32,6144]{1,0:T(8,128)S(1)}, f32[32,6144]{1,0:T(8,128)}, u32[]{:S(2)}, u32[]{:S(2)}) collective-permute-start(f32[32,6144]{1,0:T(8,128)S(1)} %collective-permute-done.1.odd2_ref), channel_id=1, source_target_pairs={{32,64},{96,128},{160,192},{224,256},{288,320},{352,384},{416,448}... | collective-permute-start | bytes 2359304 | tf_op jit(solution)/shard_map/ppermute | solution.py:16
  44.5 4.8 %all-to-all-done.got_ref = f32[16,16,128]{2,1,0:T(8,128)S(1)} async-done(((f32[16,16,128]{2,1,0:T(8,128)}), f32[16,16,128]{2,1,0:T(8,128)S(1)}, u32[]{:S(2)}, u32[]{:S(2)}) %all-to-all-start) | async-done | bytes 131104 | tf_op jit(solution)/shard_map/all_to_all | solution.py:200
  49.4 1.3 %collective-permute-start.4 = (f32[32,6144]{1,0:T(8,128)S(1)}, f32[32,6144]{1,0:T(8,128)}, u32[]{:S(2)}, u32[]{:S(2)}) collective-permute-start(f32[32,6144]{1,0:T(8,128)S(1)} %collective-permute-done.1.odd2_ref), channel_id=1, source_target_pairs={{32,0},{33,1},{34,2},{35,3},{36,4},{37,5},{38,6},{39,7},{40,8},{41... | collective-permute-start | bytes 2359304 | tf_op jit(solution)/shard_map/ppermute | solution.py:205
  50.7 4.8 %collective-permute-start.7 = (f32[32,6144]{1,0:T(8,128)}, f32[32,6144]{1,0:T(8,128)}, u32[]{:S(2)}, u32[]{:S(2)}) collective-permute-start(f32[32,6144]{1,0:T(8,128)} %collective-permute-done.2.even_ref.even2_ref), channel_id=1, source_target_pairs={{0,32},{1,33},{2,34},{3,35},{4,36},{5,37},{6,38},{7,39},{8,40},{9,... | collective-permute-start | bytes 2359304 | tf_op jit(solution)/shard_map/ppermute | solution.py:206
  55.5 21.3 %all_to_all.10.got_ref = f32[4,32,128]{2,1,0:T(8,128)S(1)} all-to-all(f32[4,32,128]{2,1,0:T(8,128)S(1)} %shard_map.29), channel_id=1, replica_groups=mesh['zl'=2,'y'=8,'core'=2,'zh'=4,'x'=8] {'zh'}, dimensions={0} | all-to-all | bytes 131072 | tf_op jit(solution)/shard_map/all_to_all | solution.py:204
  76.8 0.1 shard_map.30.inter_ref
  76.9 0.0 collective-permute-done.5.even1_ref
  76.9 4.2 %shard_map.31 = f32[32,6144]{1,0:T(8,128)} custom-call(s32[1]{0:T(128)} %bitcast.odd_ref, f32[32,128]{1,0:T(8,128)S(1)} %shard_map.30.inter_ref, f32[32,6144]{1,0:T(8,128)S(1)} %copy-done.1, f32[32,6144]{1,0:T(8,128)} %collective-permute-done.4.odd1_ref, f32[32,6144]{1,0:T(8,128)S(1)} %collective-permute-done.5.even1_ref, ...), custom_call_target="tpu_custom_call" | custom-call | tf_op jit(solution)/shard_map/pallas_call | solution.py:174
  (8 shorter events, 0.0 us)
Async XLA Ops:
  0.0 12.3 %copy-start = (f32[32,6144]{1,0:T(8,128)S(1)}, f32[32,6144]{1,0:T(8,128)}, u32[]{:S(2)}) copy-start(f32[32,6144]{1,0:T(8,128)} %h_ref.3) | copy-start | bytes 2359300
  0.0 12.2 %collective-permute-start.1 = (f32[32,6144]{1,0:T(8,128)}, f32[32,6144]{1,0:T(8,128)S(1)}, u32[]{:S(2)}, u32[]{:S(2)}) collective-permute-start(f32[32,6144]{1,0:T(8,128)} %psi_ref.1), channel_id=1, source_target_pairs={{32,96},{96,160},{160,224},{224,288},{288,352},{352,416},{416,480}... | collective-permute-start | bytes 2359304 | tf_op jit(solution)/shard_map/ppermute | solution.py:16
  0.8 19.4 %collective-permute-start = (f32[32,6144]{1,0:T(8,128)}, f32[32,6144]{1,0:T(8,128)S(1)}, u32[]{:S(2)}, u32[]{:S(2)}) collective-permute-start(f32[32,6144]{1,0:T(8,128)} %h_ref.3), channel_id=1, source_target_pairs={{0,992},{32,0},{64,32},{96,64},{128,96},{160,128},{192,160},{224,1... | collective-permute-start | bytes 2359304 | tf_op jit(solution)/shard_map/ppermute | solution.py:16
  12.2 1.1 %copy-start.1 = (f32[32,6144]{1,0:T(8,128)S(1)}, f32[32,6144]{1,0:T(8,128)}, u32[]{:S(2)}) copy-start(f32[32,6144]{1,0:T(8,128)} %psi_ref.1) | copy-start | bytes 2359300
  13.4 16.3 %collective-permute-start.2 = (f32[32,6144]{1,0:T(8,128)S(1)}, f32[32,6144]{1,0:T(8,128)}, u32[]{:S(2)}, u32[]{:S(2)}) collective-permute-start(f32[32,6144]{1,0:T(8,128)S(1)} %copy-done.1), channel_id=1, source_target_pairs={{0,64},{64,128},{128,192},{192,256},{256,320},{320,384},{384,448},... | collective-permute-start | bytes 2359304 | tf_op jit(solution)/shard_map/ppermute | solution.py:16
  21.2 0.7 collective-permute-start.3
  32.3 17.1 %all-to-all-start = ((f32[16,16,128]{2,1,0:T(8,128)}), f32[16,16,128]{2,1,0:T(8,128)S(1)}, u32[]{:S(2)}, u32[]{:S(2)}) async-start(f32[16,16,128]{2,1,0:T(8,128)} %shard_map.28), calls=%async_computation | async-start | bytes 262144 | tf_op jit(solution)/shard_map/all_to_all | solution.py:200
  41.1 35.8 %collective-permute-start.5 = (f32[32,6144]{1,0:T(8,128)S(1)}, f32[32,6144]{1,0:T(8,128)S(1)}, u32[]{:S(2)}, u32[]{:S(2)}) collective-permute-start(f32[32,6144]{1,0:T(8,128)S(1)} %copy-done.1), channel_id=1, source_target_pairs={{0,32},{1,33},{2,34},{3,35},{4,36},{5,37},{6,38},{7,39},{8,40},{9,... | collective-permute-start | bytes 2359304 | tf_op jit(solution)/shard_map/ppermute | solution.py:194
  43.2 33.7 %collective-permute-start.6 = (f32[32,6144]{1,0:T(8,128)S(1)}, f32[32,6144]{1,0:T(8,128)}, u32[]{:S(2)}, u32[]{:S(2)}) collective-permute-start(f32[32,6144]{1,0:T(8,128)S(1)} %collective-permute-done.1.odd2_ref), channel_id=1, source_target_pairs={{32,64},{96,128},{160,192},{224,256},{288,320},{352,384},{416,448}... | collective-permute-start | bytes 2359304 | tf_op jit(solution)/shard_map/ppermute | solution.py:16
  49.4 27.5 %collective-permute-start.4 = (f32[32,6144]{1,0:T(8,128)S(1)}, f32[32,6144]{1,0:T(8,128)}, u32[]{:S(2)}, u32[]{:S(2)}) collective-permute-start(f32[32,6144]{1,0:T(8,128)S(1)} %collective-permute-done.1.odd2_ref), channel_id=1, source_target_pairs={{32,0},{33,1},{34,2},{35,3},{36,4},{37,5},{38,6},{39,7},{40,8},{41... | collective-permute-start | bytes 2359304 | tf_op jit(solution)/shard_map/ppermute | solution.py:205
  50.7 26.2 %collective-permute-start.7 = (f32[32,6144]{1,0:T(8,128)}, f32[32,6144]{1,0:T(8,128)}, u32[]{:S(2)}, u32[]{:S(2)}) collective-permute-start(f32[32,6144]{1,0:T(8,128)} %collective-permute-done.2.even_ref.even2_ref), channel_id=1, source_target_pairs={{0,32},{1,33},{2,34},{3,35},{4,36},{5,37},{6,38},{7,39},{8,40},{9,... | collective-permute-start | bytes 2359304 | tf_op jit(solution)/shard_map/ppermute | solution.py:206

commit v4 on v3

--- a/solution.py
+++ b/solution.py
@@ -51,6 +51,7 @@
 
 SCALAR = pl.BlockSpec(memory_space=pltpu.SMEM)
 VECTOR = pl.BlockSpec(memory_space=pltpu.VMEM)
+ANYWHERE = pl.BlockSpec(memory_space=pl.ANY)
 PARAMS = pltpu.CompilerParams(vmem_limit_bytes=40 << 20)
 
 
@@ -58,7 +59,9 @@
     return [pltpu.with_memory_space_constraint(x, pltpu.VMEM) for x in arrays]
 
 
-def slots_kernel(odd_ref, h_ref, a_ref, even_ref, own_ref, ahead_ref, own_odd_ref, hop_ref, out_ref):
+def slots_kernel(
+    odd_ref, h_ref, a_ref, even_ref, own_ref, ahead_ref, own_odd_ref, hop_ref, out_ref, wide, sems
+):
     half = out_ref.shape[0] // 2
 
     def put(start, left, right):
@@ -68,13 +71,25 @@
 
     @pl.when(odd_ref[0] == 0)
     def _():
-        step = h_ref.shape[1] // 4
+        steps = sems.shape[0]
+        step = wide.shape[2] // steps
+        spans = [pl.ds(k * step, step) for k in range(steps)]
+        loads = [
+            [
+                pltpu.make_async_copy(ref.at[:, at], wide.at[n, :, at], sems.at[k, n])
+                for n, ref in enumerate((h_ref, a_ref, even_ref))
+            ]
+            for k, at in enumerate(spans)
+        ]
+        for load in loads:
+            for copy in load:
+                copy.start()
         late = jnp.zeros((64, 32), jnp.float32)
-        for k in range(4):
-            at = pl.ds(k * step, step)
-            late += product(
-                jnp.concatenate([h_ref[:, at], a_ref[:, at]], 0), even_ref[:, at], ((1,), (1,))
-            )
+        for load, at in zip(loads, spans):
+            for copy in load:
+                copy.wait()
+            left = jnp.concatenate([wide[0, :, at], wide[1, :, at]], 0)
+            late += product(left, wide[2, :, at], ((1,), (1,)))
         put(0, own_ref[...], late[:32])
         put(half, ahead_ref[...], late[32:])
 
@@ -88,8 +103,12 @@
     return pl.pallas_call(
         slots_kernel,
         out_shape=jax.ShapeDtypeStruct((count, 16, 128), jnp.float32),
-        in_specs=[SCALAR] + [VECTOR] * 7,
+        in_specs=[SCALAR] + [ANYWHERE] * 3 + [VECTOR] * 4,
         out_specs=VECTOR,
+        scratch_shapes=[
+            pltpu.VMEM((3,) + wide[0].shape, jnp.float32),
+            pltpu.SemaphoreType.DMA((4, 3)),
+        ],
         compiler_params=PARAMS,
     )(odd, *near(*wide), *small)
 
@@ -129,32 +148,37 @@
         in_specs=[SCALAR, VECTOR],
         out_specs=VECTOR,
         cost_estimate=pl.CostEstimate(
-            flops=5_000_000_000, bytes_accessed=1024, transcendentals=0
+            flops=8_000_000_000, bytes_accessed=1024, transcendentals=0
         ),
     )(odd, *near(got))
 
 
 def finish_kernel(
     odd_ref, inter_ref, psi_ref, odd1_ref, even1_ref, odd2_ref, even2_ref, odd3_ref, even3_ref, h_ref,
-    out_ref, h, made, into, out
+    out_ref, wide, made, into, out
 ):
-    steps = into.shape[0]
-    step = h.shape[1] // steps
-    loads = []
-    for k in range(steps):
-        at = pl.ds(k * step, step)
-        loads.append(pltpu.make_async_copy(h_ref.at[:, at], h.at[:, at], into.at[k]))
-        loads[-1].start()
-    inter = inter_ref[...]
-
-    def finish(*behind):
+    steps = out.shape[0]
+    step = made.shape[1] // steps
+    spans = [pl.ds(k * step, step) for k in range(steps)]
+
+    def finish(*refs):
+        loads = [
+            [
+                pltpu.make_async_copy(ref.at[:, at], wide.at[n, :, at], into.at[k, n])
+                for n, ref in enumerate(refs)
+            ]
+            for k, at in enumerate(spans)
+        ]
+        for load in loads:
+            for copy in load:
+                copy.start()
+        inter = inter_ref[...]
         stores = []
-        for k in range(steps):
-            at = pl.ds(k * step, step)
-            window = jnp.concatenate([ref[:, at] for ref in (psi_ref,) + behind], 0)
-            shift = product(inter, window, ((1,), (0,)))
-            loads[k].wait()
-            made[:, at] = h[:, at] - shift
+        for k, at in enumerate(spans):
+            for copy in loads[k]:
+                copy.wait()
+            window = jnp.concatenate([wide[n, :, at] for n in range(1, 5)], 0)
+            made[:, at] = wide[0, :, at] - product(inter, window, ((1,), (0,)))
             stores.append(pltpu.make_async_copy(made.at[:, at], out_ref.at[:, at], out.at[k]))
             stores[-1].start()
         for copy in stores:
@@ -162,21 +186,26 @@
 
     @pl.when(odd_ref[0] == 0)
     def _():
-        finish(even2_ref, odd1_ref, odd3_ref)
+        finish(h_ref, psi_ref, even2_ref, odd1_ref, odd3_ref)
 
     @pl.when(odd_ref[0] == 1)
     def _():
-        finish(odd2_ref, even1_ref, even3_ref)
+        finish(h_ref, psi_ref, odd2_ref, even1_ref, even3_ref)
 
 
 def finished(odd, inter, blocks, hpsi):
-    block = pltpu.VMEM(hpsi.shape, jnp.float32)
+    shape = hpsi.shape
     return pl.pallas_call(
         finish_kernel,
-        out_shape=jax.ShapeDtypeStruct(hpsi.shape, jnp.float32),
-        in_specs=[SCALAR] + [VECTOR] * 8 + [pl.BlockSpec(memory_space=pl.ANY)],
-        out_specs=pl.BlockSpec(memory_space=pl.ANY),
-        scratch_shapes=[block, block, pltpu.SemaphoreType.DMA((6,)), pltpu.SemaphoreType.DMA((6,))],
+        out_shape=jax.ShapeDtypeStruct(shape, jnp.float32),
+        in_specs=[SCALAR, VECTOR] + [ANYWHERE] * 8,
+        out_specs=ANYWHERE,
+        scratch_shapes=[
+            pltpu.VMEM((5,) + shape, jnp.float32),
+            pltpu.VMEM(shape, jnp.float32),
+            pltpu.SemaphoreType.DMA((6, 5)),
+            pltpu.SemaphoreType.DMA((6,)),
+        ],
         compiler_params=PARAMS,
     )(odd, *near(inter, *blocks), hpsi)
 
@@ -204,6 +233,7 @@
     got = lax.all_to_all(line, "zh", 0, 0, tiled=True)
     odd1 = lax.ppermute(odd2_last, "core", [(1, 0)])
     even3 = lax.ppermute(even2_last, "core", [(0, 1)])
+    got, odd3, even1 = lax.optimization_barrier((got, odd3, even1))
     inter = total_of(odd, got)
     return finished(odd, inter, (psi, odd1, even1, odd2, even2, odd3, even3), hpsi)
 

time: 81.7 us -> 76.5 us (0.936)
  the two profiles are of different devices: /device:TPU:2 before, /device:TPU:1 now
where the time goes in v4:
time: 76.5 us; the launch traced here: 76 us
  starting transfers between devices  49.5 us (65%)
  waiting for transfers between devices  17.9 us (23%)
  Pallas kernels  4.97 us (6%)
  matrix products  3.22 us (4%)
    ppermute x5, starting transfers between devices, shifted(): return lax.ppermute(value, BAND, pairs)  22.5 us
    all_to_all x1, starting transfers between devices, on_device(): got = lax.all_to_all(line, 'zh', 0, 0, tiled=True)  12.9 us
    ppermute x5, waiting for transfers between devices, shifted(): return lax.ppermute(value, BAND, pairs)  10.9 us
    all_to_all x1, starting transfers between devices, on_device(): got = lax.all_to_all(slots, ('core', 'x'), 0, 0, tiled=True)  7.1 us
    ppermute x1, starting transfers between devices, on_device(): odd1 = lax.ppermute(odd2_last, 'core', [(1, 0)])  4.37 us
    all_to_all x1, waiting for transfers between devices, on_device(): got = lax.all_to_all(slots, ('core', 'x'), 0, 0, tiled=True)  3.9 us
    pallas_call x1, Pallas kernels, finished(): pl.pallas_call(finish_kernel, out_shape=jax.ShapeDtypeStruct(shape, jnp.f...  3.34 us
    dot_general x4, matrix products, overlap(): lax.dot_general(h, psi, (((1,), (1,)), ((), ())), precision=PRECISION, pr...  3.22 us
  transfers between devices with their start and end apart: 10, of which 5 were waited for; matrix products, arithmetic and copies ran while one was open for 4% of the time, Pallas kernels for 1%

profile of v4, /device:TPU:1, one launch (start us, length us, event | category | flops | bytes accessed | tf_op | source)
XLA Modules:
  0.0 76.0 jit_solution(2108215503075319143)
XLA Ops:
  0.0 4.3 %collective-permute-start.1 = (f32[32,6144]{1,0:T(8,128)}, f32[32,6144]{1,0:T(8,128)S(1)}, u32[]{:S(2)}, u32[]{:S(2)}) collective-permute-start(f32[32,6144]{1,0:T(8,128)} %psi_ref.1), channel_id=1, source_target_pairs={{32,96},{96,160},{160,224},{224,288},{288,352},{352,416},{416,480}... | collective-permute-start | bytes 2359304 | tf_op jit(solution)/shard_map/ppermute | solution.py:16
  4.3 12.6 %collective-permute-start = (f32[32,6144]{1,0:T(8,128)}, f32[32,6144]{1,0:T(8,128)S(1)}, u32[]{:S(2)}, u32[]{:S(2)}) collective-permute-start(f32[32,6144]{1,0:T(8,128)} %h_ref.3), channel_id=1, source_target_pairs={{0,992},{32,0},{64,32},{96,64},{128,96},{160,128},{192,160},{224,1... | collective-permute-start | bytes 2359304 | tf_op jit(solution)/shard_map/ppermute | solution.py:16
  16.9 1.8 %fusion.own_ref = f32[32,32]{1,0:T(8,128)S(1)} fusion(f32[32,6144]{1,0:T(8,128)} %h_ref.3, f32[32,6144]{1,0:T(8,128)} %psi_ref.1), kind=kOutput, calls=%fused_computation.1 | convolution fusion | flops 37748736 | bytes 1576960 | tf_op jit(solution)/shard_map/dot_general | solution.py:20
  18.8 0.4 collective-permute-done.1.odd2_ref
  19.2 0.5 fusion.1.own_odd_ref
  19.6 0.3 copy-done.1
  19.9 1.6 %collective-permute-start.2 = (f32[32,6144]{1,0:T(8,128)S(1)}, f32[32,6144]{1,0:T(8,128)}, u32[]{:S(2)}, u32[]{:S(2)}) collective-permute-start(f32[32,6144]{1,0:T(8,128)S(1)} %copy-done.1), channel_id=1, source_target_pairs={{0,64},{64,128},{128,192},{192,256},{256,320},{320,384},{384,448},... | collective-permute-start | bytes 2359304 | tf_op jit(solution)/shard_map/ppermute | solution.py:16
  21.4 0.5 fusion.2.ahead_ref
  21.9 0.5 fusion.3
  22.5 1.9 %collective-permute-start.3 = (f32[32,64]{1,0:T(8,128)S(1)}, f32[32,64]{1,0:T(8,128)S(1)}, u32[]{:S(2)}, u32[]{:S(2)}) collective-permute-start(f32[32,64]{1,0:T(8,128)S(1)} %pad_maximum_fusion), channel_id=1, source_target_pairs={{32,96},{96,160},{160,224},{224,288},{288,352},{352,416},{416,480}... | collective-permute-start | bytes 24584 | tf_op jit(solution)/shard_map/ppermute | solution.py:16
  24.4 10.5 %collective-permute-done.3.hop_ref = f32[32,64]{1,0:T(8,128)S(1)} collective-permute-done((f32[32,64]{1,0:T(8,128)S(1)}, f32[32,64]{1,0:T(8,128)S(1)}, u32[]{:S(2)}, u32[]{:S(2)}) %collective-permute-start.3) | collective-permute-done | bytes 8224 | tf_op jit(solution)/shard_map/ppermute | solution.py:16
  34.9 0.8 %shard_map.28 = f32[16,16,128]{2,1,0:T(8,128)} custom-call(s32[1]{0:T(128)} %bitcast.odd_ref, f32[32,6144]{1,0:T(8,128)S(1)} %copy-done, f32[32,6144]{1,0:T(8,128)S(1)} %collective-permute-done.a_ref, f32[32,6144]{1,0:T(8,128)} %collective-permute-done.2.even_ref.even2_ref, f32[32,32]{1,0:T(8,128)S(1)} %fusion.own_ref, f32[32,32]{1,0:T(8,128)S(1)} %fusion.2.ahead_ref, ...), custom_call_target="tpu_custom_call" | custom-call | tf_op jit(solution)/shard_map/pallas_call | solution.py:103
  35.8 7.1 %all-to-all-start = ((f32[16,16,128]{2,1,0:T(8,128)}), f32[16,16,128]{2,1,0:T(8,128)S(1)}, u32[]{:S(2)}, u32[]{:S(2)}) async-start(f32[16,16,128]{2,1,0:T(8,128)} %shard_map.28), calls=%async_computation | async-start | bytes 262144 | tf_op jit(solution)/shard_map/all_to_all | solution.py:229
  42.9 1.3 %collective-permute-start.5 = (f32[32,6144]{1,0:T(8,128)S(1)}, f32[32,6144]{1,0:T(8,128)S(1)}, u32[]{:S(2)}, u32[]{:S(2)}) collective-permute-start(f32[32,6144]{1,0:T(8,128)S(1)} %copy-done.1), channel_id=1, source_target_pairs={{0,32},{1,33},{2,34},{3,35},{4,36},{5,37},{6,38},{7,39},{8,40},{9,... | collective-permute-start | bytes 2359304 | tf_op jit(solution)/shard_map/ppermute | solution.py:223
  44.2 2.2 %collective-permute-start.4 = (f32[32,6144]{1,0:T(8,128)S(1)}, f32[32,6144]{1,0:T(8,128)}, u32[]{:S(2)}, u32[]{:S(2)}) collective-permute-start(f32[32,6144]{1,0:T(8,128)S(1)} %collective-permute-done.1.odd2_ref), channel_id=1, source_target_pairs={{32,64},{96,128},{160,192},{224,256},{288,320},{352,384},{416,448}... | collective-permute-start | bytes 2359304 | tf_op jit(solution)/shard_map/ppermute | solution.py:16
  46.3 3.9 %all-to-all-done.got_ref = f32[16,16,128]{2,1,0:T(8,128)S(1)} async-done(((f32[16,16,128]{2,1,0:T(8,128)}), f32[16,16,128]{2,1,0:T(8,128)S(1)}, u32[]{:S(2)}, u32[]{:S(2)}) %all-to-all-start) | async-done | bytes 131104 | tf_op jit(solution)/shard_map/all_to_all | solution.py:229
  50.2 0.6 shard_map.29
  50.9 12.9 %all-to-all-start.1 = ((f32[4,32,128]{2,1,0:T(8,128)}), f32[4,32,128]{2,1,0:T(8,128)S(1)}, u32[]{:S(2)}, u32[]{:S(2)}) async-start(f32[4,32,128]{2,1,0:T(8,128)} %shard_map.29), calls=%async_computation.1 | async-start | bytes 131072 | tf_op jit(solution)/shard_map/all_to_all | solution.py:233
  63.8 4.4 %collective-permute-start.6 = (f32[32,6144]{1,0:T(8,128)S(1)}, f32[32,6144]{1,0:T(8,128)}, u32[]{:S(2)}, u32[]{:S(2)}) collective-permute-start(f32[32,6144]{1,0:T(8,128)S(1)} %collective-permute-done.1.odd2_ref), channel_id=1, source_target_pairs={{32,0},{33,1},{34,2},{35,3},{36,4},{37,5},{38,6},{39,7},{40,8},{41... | collective-permute-start | bytes 2359304 | tf_op jit(solution)/shard_map/ppermute | solution.py:234
  68.2 1.3 %collective-permute-start.7 = (f32[32,6144]{1,0:T(8,128)}, f32[32,6144]{1,0:T(8,128)}, u32[]{:S(2)}, u32[]{:S(2)}) collective-permute-start(f32[32,6144]{1,0:T(8,128)} %collective-permute-done.2.even_ref.even2_ref), channel_id=1, source_target_pairs={{0,32},{1,33},{2,34},{3,35},{4,36},{5,37},{6,38},{7,39},{8,40},{9,... | collective-permute-start | bytes 2359304 | tf_op jit(solution)/shard_map/ppermute | solution.py:235
  69.5 1.6 %all-to-all-done.1.got_ref = f32[4,32,128]{2,1,0:T(8,128)S(1)} async-done(((f32[4,32,128]{2,1,0:T(8,128)}), f32[4,32,128]{2,1,0:T(8,128)S(1)}, u32[]{:S(2)}, u32[]{:S(2)}) %all-to-all-start.1) | async-done | bytes 65568 | tf_op jit(solution)/shard_map/all_to_all | solution.py:233
  71.0 0.1 shard_map.30.inter_ref
  71.2 1.5 %collective-permute-done.7.even3_ref = f32[32,6144]{1,0:T(8,128)} collective-permute-done((f32[32,6144]{1,0:T(8,128)}, f32[32,6144]{1,0:T(8,128)}, u32[]{:S(2)}, u32[]{:S(2)}) %collective-permute-start.7) | collective-permute-done | bytes 786464 | tf_op jit(solution)/shard_map/ppermute | solution.py:235
  72.7 3.3 %shard_map.31 = f32[32,6144]{1,0:T(8,128)} custom-call(s32[1]{0:T(128)} %bitcast.odd_ref, f32[32,128]{1,0:T(8,128)S(1)} %shard_map.30.inter_ref, f32[32,6144]{1,0:T(8,128)S(1)} %copy-done.1, f32[32,6144]{1,0:T(8,128)} %collective-permute-done.6.odd1_ref, f32[32,6144]{1,0:T(8,128)S(1)} %collective-permute-done.5.even1_ref, ...), custom_call_target="tpu_custom_call" | custom-call | tf_op jit(solution)/shard_map/pallas_call | solution.py:198
  (9 shorter events, 0.1 us)
Async XLA Ops:
  0.0 19.1 %copy-start = (f32[32,6144]{1,0:T(8,128)S(1)}, f32[32,6144]{1,0:T(8,128)}, u32[]{:S(2)}) copy-start(f32[32,6144]{1,0:T(8,128)} %h_ref.3) | copy-start | bytes 2359300
  0.0 19.1 %collective-permute-start.1 = (f32[32,6144]{1,0:T(8,128)}, f32[32,6144]{1,0:T(8,128)S(1)}, u32[]{:S(2)}, u32[]{:S(2)}) collective-permute-start(f32[32,6144]{1,0:T(8,128)} %psi_ref.1), channel_id=1, source_target_pairs={{32,96},{96,160},{160,224},{224,288},{288,352},{352,416},{416,480}... | collective-permute-start | bytes 2359304 | tf_op jit(solution)/shard_map/ppermute | solution.py:16
  4.3 17.2 %collective-permute-start = (f32[32,6144]{1,0:T(8,128)}, f32[32,6144]{1,0:T(8,128)S(1)}, u32[]{:S(2)}, u32[]{:S(2)}) collective-permute-start(f32[32,6144]{1,0:T(8,128)} %h_ref.3), channel_id=1, source_target_pairs={{0,992},{32,0},{64,32},{96,64},{128,96},{160,128},{192,160},{224,1... | collective-permute-start | bytes 2359304 | tf_op jit(solution)/shard_map/ppermute | solution.py:16
  18.7 1.1 %copy-start.1 = (f32[32,6144]{1,0:T(8,128)S(1)}, f32[32,6144]{1,0:T(8,128)}, u32[]{:S(2)}) copy-start(f32[32,6144]{1,0:T(8,128)} %psi_ref.1) | copy-start | bytes 2359300
  19.9 15.0 %collective-permute-start.2 = (f32[32,6144]{1,0:T(8,128)S(1)}, f32[32,6144]{1,0:T(8,128)}, u32[]{:S(2)}, u32[]{:S(2)}) collective-permute-start(f32[32,6144]{1,0:T(8,128)S(1)} %copy-done.1), channel_id=1, source_target_pairs={{0,64},{64,128},{128,192},{192,256},{256,320},{320,384},{384,448},... | collective-permute-start | bytes 2359304 | tf_op jit(solution)/shard_map/ppermute | solution.py:16
  22.5 12.5 %collective-permute-start.3 = (f32[32,64]{1,0:T(8,128)S(1)}, f32[32,64]{1,0:T(8,128)S(1)}, u32[]{:S(2)}, u32[]{:S(2)}) collective-permute-start(f32[32,64]{1,0:T(8,128)S(1)} %pad_maximum_fusion), channel_id=1, source_target_pairs={{32,96},{96,160},{160,224},{224,288},{288,352},{352,416},{416,480}... | collective-permute-start | bytes 24584 | tf_op jit(solution)/shard_map/ppermute | solution.py:16
  35.8 14.5 %all-to-all-start = ((f32[16,16,128]{2,1,0:T(8,128)}), f32[16,16,128]{2,1,0:T(8,128)S(1)}, u32[]{:S(2)}, u32[]{:S(2)}) async-start(f32[16,16,128]{2,1,0:T(8,128)} %shard_map.28), calls=%async_computation | async-start | bytes 262144 | tf_op jit(solution)/shard_map/all_to_all | solution.py:229
  42.9 26.6 %collective-permute-start.5 = (f32[32,6144]{1,0:T(8,128)S(1)}, f32[32,6144]{1,0:T(8,128)S(1)}, u32[]{:S(2)}, u32[]{:S(2)}) collective-permute-start(f32[32,6144]{1,0:T(8,128)S(1)} %copy-done.1), channel_id=1, source_target_pairs={{0,32},{1,33},{2,34},{3,35},{4,36},{5,37},{6,38},{7,39},{8,40},{9,... | collective-permute-start | bytes 2359304 | tf_op jit(solution)/shard_map/ppermute | solution.py:223
  44.2 26.9 %collective-permute-start.4 = (f32[32,6144]{1,0:T(8,128)S(1)}, f32[32,6144]{1,0:T(8,128)}, u32[]{:S(2)}, u32[]{:S(2)}) collective-permute-start(f32[32,6144]{1,0:T(8,128)S(1)} %collective-permute-done.1.odd2_ref), channel_id=1, source_target_pairs={{32,64},{96,128},{160,192},{224,256},{288,320},{352,384},{416,448}... | collective-permute-start | bytes 2359304 | tf_op jit(solution)/shard_map/ppermute | solution.py:16
  50.9 20.1 %all-to-all-start.1 = ((f32[4,32,128]{2,1,0:T(8,128)}), f32[4,32,128]{2,1,0:T(8,128)S(1)}, u32[]{:S(2)}, u32[]{:S(2)}) async-start(f32[4,32,128]{2,1,0:T(8,128)} %shard_map.29), calls=%async_computation.1 | async-start | bytes 131072 | tf_op jit(solution)/shard_map/all_to_all | solution.py:233
  63.8 7.4 %collective-permute-start.6 = (f32[32,6144]{1,0:T(8,128)S(1)}, f32[32,6144]{1,0:T(8,128)}, u32[]{:S(2)}, u32[]{:S(2)}) collective-permute-start(f32[32,6144]{1,0:T(8,128)S(1)} %collective-permute-done.1.odd2_ref), channel_id=1, source_target_pairs={{32,0},{33,1},{34,2},{35,3},{36,4},{37,5},{38,6},{39,7},{40,8},{41... | collective-permute-start | bytes 2359304 | tf_op jit(solution)/shard_map/ppermute | solution.py:234
  68.2 4.5 %collective-permute-start.7 = (f32[32,6144]{1,0:T(8,128)}, f32[32,6144]{1,0:T(8,128)}, u32[]{:S(2)}, u32[]{:S(2)}) collective-permute-start(f32[32,6144]{1,0:T(8,128)} %collective-permute-done.2.even_ref.even2_ref), channel_id=1, source_target_pairs={{0,32},{1,33},{2,34},{3,35},{4,36},{5,37},{6,38},{7,39},{8,40},{9,... | collective-permute-start | bytes 2359304 | tf_op jit(solution)/shard_map/ppermute | solution.py:235

commit v5 on v4

--- a/solution.py
+++ b/solution.py
@@ -60,7 +60,7 @@
 
 
 def slots_kernel(
-    odd_ref, h_ref, a_ref, even_ref, own_ref, ahead_ref, own_odd_ref, hop_ref, out_ref, wide, sems
+    odd_ref, h_ref, a_ref, even_ref, own_ref, ahead_ref, own_odd_ref, hop_ref, out_ref, late_ref, sems
 ):
     half = out_ref.shape[0] // 2
 
@@ -72,24 +72,19 @@
     @pl.when(odd_ref[0] == 0)
     def _():
         steps = sems.shape[0]
-        step = wide.shape[2] // steps
+        step = late_ref.shape[1] // steps
         spans = [pl.ds(k * step, step) for k in range(steps)]
         loads = [
-            [
-                pltpu.make_async_copy(ref.at[:, at], wide.at[n, :, at], sems.at[k, n])
-                for n, ref in enumerate((h_ref, a_ref, even_ref))
-            ]
+            pltpu.make_async_copy(even_ref.at[:, at], late_ref.at[:, at], sems.at[k])
             for k, at in enumerate(spans)
         ]
         for load in loads:
-            for copy in load:
-                copy.start()
+            load.start()
         late = jnp.zeros((64, 32), jnp.float32)
         for load, at in zip(loads, spans):
-            for copy in load:
-                copy.wait()
-            left = jnp.concatenate([wide[0, :, at], wide[1, :, at]], 0)
-            late += product(left, wide[2, :, at], ((1,), (1,)))
+            load.wait()
+            left = jnp.concatenate([h_ref[:, at], a_ref[:, at]], 0)
+            late += product(left, late_ref[:, at], ((1,), (1,)))
         put(0, own_ref[...], late[:32])
         put(half, ahead_ref[...], late[32:])
 
@@ -103,11 +98,11 @@
     return pl.pallas_call(
         slots_kernel,
         out_shape=jax.ShapeDtypeStruct((count, 16, 128), jnp.float32),
-        in_specs=[SCALAR] + [ANYWHERE] * 3 + [VECTOR] * 4,
+        in_specs=[SCALAR, VECTOR, VECTOR, ANYWHERE] + [VECTOR] * 4,
         out_specs=VECTOR,
         scratch_shapes=[
-            pltpu.VMEM((3,) + wide[0].shape, jnp.float32),
-            pltpu.SemaphoreType.DMA((4, 3)),
+            pltpu.VMEM(wide[0].shape, jnp.float32),
+            pltpu.SemaphoreType.DMA((4,)),
         ],
         compiler_params=PARAMS,
     )(odd, *near(*wide), *small)
@@ -220,20 +215,21 @@
 
     ahead, ahead_odd = overlap(ahead1, psi), overlap(ahead1, odd2)
     hopped = shifted(jnp.concatenate([ahead, ahead_odd], 1), 2, 1, 2)
-    even1 = lax.ppermute(psi, "core", [(0, 1)])
 
     slots = slots_of(
         odd, (hpsi, ahead1, even2), (own, ahead, own_odd, hopped), 2 * lax.axis_size("x")
     )
-    slots, odd2_later = lax.optimization_barrier((slots, odd2))
+    slots, odd2_later, psi_later = lax.optimization_barrier((slots, odd2, psi))
     got = lax.all_to_all(slots, ("core", "x"), 0, 0, tiled=True)
     odd3 = shifted(odd2_later, 1, 1, 2)
+    even1 = lax.ppermute(psi_later, "core", [(0, 1)])
     line = line_of(got, lax.axis_size("zh"))
     line, odd2_last, even2_last = lax.optimization_barrier((line, odd2, even2))
     got = lax.all_to_all(line, "zh", 0, 0, tiled=True)
     odd1 = lax.ppermute(odd2_last, "core", [(1, 0)])
     even3 = lax.ppermute(even2_last, "core", [(0, 1)])
-    got, odd3, even1 = lax.optimization_barrier((got, odd3, even1))
+    got, odd3 = lax.optimization_barrier((got, odd3))
+    got, even1 = lax.optimization_barrier((got, even1))
     inter = total_of(odd, got)
     return finished(odd, inter, (psi, odd1, even1, odd2, even2, odd3, even3), hpsi)
 

time: 76.5 us -> 76.4 us (level)
  starting transfers between devices: 49.5 us -> 48.5 us
  waiting for transfers between devices: 17.9 us -> 18.7 us
    ppermute x5, starting transfers between devices: 22.5 us -> 21.7 us  [shifted(): return lax.ppermute(value, BAND, pairs)]
    all_to_all x1, waiting for transfers between devices: 3.9 us -> 4.72 us  [on_device(): got = lax.all_to_all(slots, ('core', 'x'), 0, 0, tiled=True)]
where the time goes in v5:
time: 76.4 us; the launch traced here: 75.8 us
  starting transfers between devices  48.5 us (63%)
  waiting for transfers between devices  18.7 us (24%)
  Pallas kernels  4.92 us (6%)
  matrix products  3.22 us (4%)
    ppermute x5, starting transfers between devices, shifted(): return lax.ppermute(value, BAND, pairs)  21.7 us
    all_to_all x1, starting transfers between devices, on_device(): got = lax.all_to_all(line, 'zh', 0, 0, tiled=True)  12.9 us
    ppermute x5, waiting for transfers between devices, shifted(): return lax.ppermute(value, BAND, pairs)  10.9 us
    all_to_all x1, starting transfers between devices, on_device(): got = lax.all_to_all(slots, ('core', 'x'), 0, 0, tiled=True)  6.97 us
    all_to_all x1, waiting for transfers between devices, on_device(): got = lax.all_to_all(slots, ('core', 'x'), 0, 0, tiled=True)  4.72 us
    ppermute x1, starting transfers between devices, on_device(): odd1 = lax.ppermute(odd2_last, 'core', [(1, 0)])  4.37 us
    pallas_call x1, Pallas kernels, finished(): pl.pallas_call(finish_kernel, out_shape=jax.ShapeDtypeStruct(shape, jnp.f...  3.36 us
    dot_general x4, matrix products, overlap(): lax.dot_general(h, psi, (((1,), (1,)), ((), ())), precision=PRECISION, pr...  3.22 us
  transfers between devices with their start and end apart: 10, of which 5 were waited for; matrix products, arithmetic and copies ran while one was open for 4% of the time, Pallas kernels for 1%

profile of v5, /device:TPU:1, one launch (start us, length us, event | category | flops | bytes accessed | tf_op | source)
XLA Modules:
  0.0 75.8 jit_solution(821212834523744170)
XLA Ops:
  0.0 4.3 %collective-permute-start.1 = (f32[32,6144]{1,0:T(8,128)}, f32[32,6144]{1,0:T(8,128)S(1)}, u32[]{:S(2)}, u32[]{:S(2)}) collective-permute-start(f32[32,6144]{1,0:T(8,128)} %psi_ref.1), channel_id=1, source_target_pairs={{32,96},{96,160},{160,224},{224,288},{288,352},{352,416},{416,480}... | collective-permute-start | bytes 2359304 | tf_op jit(solution)/shard_map/ppermute | solution.py:16
  4.3 12.6 %collective-permute-start = (f32[32,6144]{1,0:T(8,128)}, f32[32,6144]{1,0:T(8,128)S(1)}, u32[]{:S(2)}, u32[]{:S(2)}) collective-permute-start(f32[32,6144]{1,0:T(8,128)} %h_ref.3), channel_id=1, source_target_pairs={{0,992},{32,0},{64,32},{96,64},{128,96},{160,128},{192,160},{224,1... | collective-permute-start | bytes 2359304 | tf_op jit(solution)/shard_map/ppermute | solution.py:16
  16.9 1.8 %fusion.own_ref = f32[32,32]{1,0:T(8,128)S(1)} fusion(f32[32,6144]{1,0:T(8,128)} %h_ref.3, f32[32,6144]{1,0:T(8,128)} %psi_ref.1), kind=kOutput, calls=%fused_computation.1 | convolution fusion | flops 37748736 | bytes 1576960 | tf_op jit(solution)/shard_map/dot_general | solution.py:20
  18.8 0.4 collective-permute-done.1.odd2_ref
  19.2 0.5 fusion.1.own_odd_ref
  19.6 0.3 copy-done.1
  19.9 1.6 %collective-permute-start.2 = (f32[32,6144]{1,0:T(8,128)S(1)}, f32[32,6144]{1,0:T(8,128)}, u32[]{:S(2)}, u32[]{:S(2)}) collective-permute-start(f32[32,6144]{1,0:T(8,128)S(1)} %copy-done.1), channel_id=1, source_target_pairs={{0,64},{64,128},{128,192},{192,256},{256,320},{320,384},{384,448},... | collective-permute-start | bytes 2359304 | tf_op jit(solution)/shard_map/ppermute | solution.py:16
  21.4 0.5 fusion.2.ahead_ref
  21.9 0.5 fusion.3
  22.5 1.9 %collective-permute-start.3 = (f32[32,64]{1,0:T(8,128)S(1)}, f32[32,64]{1,0:T(8,128)S(1)}, u32[]{:S(2)}, u32[]{:S(2)}) collective-permute-start(f32[32,64]{1,0:T(8,128)S(1)} %pad_maximum_fusion), channel_id=1, source_target_pairs={{32,96},{96,160},{160,224},{224,288},{288,352},{352,416},{416,480}... | collective-permute-start | bytes 24584 | tf_op jit(solution)/shard_map/ppermute | solution.py:16
  24.4 10.5 %collective-permute-done.3.hop_ref = f32[32,64]{1,0:T(8,128)S(1)} collective-permute-done((f32[32,64]{1,0:T(8,128)S(1)}, f32[32,64]{1,0:T(8,128)S(1)}, u32[]{:S(2)}, u32[]{:S(2)}) %collective-permute-start.3) | collective-permute-done | bytes 8224 | tf_op jit(solution)/shard_map/ppermute | solution.py:16
  34.9 0.8 %shard_map.28 = f32[16,16,128]{2,1,0:T(8,128)} custom-call(s32[1]{0:T(128)} %bitcast.odd_ref, f32[32,6144]{1,0:T(8,128)S(1)} %copy-done, f32[32,6144]{1,0:T(8,128)S(1)} %collective-permute-done.a_ref, f32[32,6144]{1,0:T(8,128)} %collective-permute-done.2.even_ref.even2_ref, f32[32,32]{1,0:T(8,128)S(1)} %fusion.own_ref, f32[32,32]{1,0:T(8,128)S(1)} %fusion.2.ahead_ref, ...), custom_call_target="tpu_custom_call" | custom-call | tf_op jit(solution)/shard_map/pallas_call | solution.py:98
  35.7 7.0 %all-to-all-start = ((f32[16,16,128]{2,1,0:T(8,128)}), f32[16,16,128]{2,1,0:T(8,128)S(1)}, u32[]{:S(2)}, u32[]{:S(2)}) async-start(f32[16,16,128]{2,1,0:T(8,128)} %shard_map.28), calls=%async_computation | async-start | bytes 262144 | tf_op jit(solution)/shard_map/all_to_all | solution.py:223
  42.7 1.3 %collective-permute-start.4 = (f32[32,6144]{1,0:T(8,128)S(1)}, f32[32,6144]{1,0:T(8,128)S(1)}, u32[]{:S(2)}, u32[]{:S(2)}) collective-permute-start(f32[32,6144]{1,0:T(8,128)S(1)} %collective-permute-done.1.odd2_ref), channel_id=1, source_target_pairs={{32,64},{96,128},{160,192},{224,256},{288,320},{352,384},{416,448}... | collective-permute-start | bytes 2359304 | tf_op jit(solution)/shard_map/ppermute | solution.py:16
  44.0 1.3 %collective-permute-start.5 = (f32[32,6144]{1,0:T(8,128)S(1)}, f32[32,6144]{1,0:T(8,128)}, u32[]{:S(2)}, u32[]{:S(2)}) collective-permute-start(f32[32,6144]{1,0:T(8,128)S(1)} %copy-done.1), channel_id=1, source_target_pairs={{0,32},{1,33},{2,34},{3,35},{4,36},{5,37},{6,38},{7,39},{8,40},{9,... | collective-permute-start | bytes 2359304 | tf_op jit(solution)/shard_map/ppermute | solution.py:225
  45.3 4.7 %all-to-all-done.got_ref = f32[16,16,128]{2,1,0:T(8,128)S(1)} async-done(((f32[16,16,128]{2,1,0:T(8,128)}), f32[16,16,128]{2,1,0:T(8,128)S(1)}, u32[]{:S(2)}, u32[]{:S(2)}) %all-to-all-start) | async-done | bytes 131104 | tf_op jit(solution)/shard_map/all_to_all | solution.py:223
  50.0 0.6 shard_map.29
  50.7 12.9 %all-to-all-start.1 = ((f32[4,32,128]{2,1,0:T(8,128)}), f32[4,32,128]{2,1,0:T(8,128)S(1)}, u32[]{:S(2)}, u32[]{:S(2)}) async-start(f32[4,32,128]{2,1,0:T(8,128)} %shard_map.29), calls=%async_computation.1 | async-start | bytes 131072 | tf_op jit(solution)/shard_map/all_to_all | solution.py:228
  63.6 4.4 %collective-permute-start.6 = (f32[32,6144]{1,0:T(8,128)S(1)}, f32[32,6144]{1,0:T(8,128)}, u32[]{:S(2)}, u32[]{:S(2)}) collective-permute-start(f32[32,6144]{1,0:T(8,128)S(1)} %collective-permute-done.1.odd2_ref), channel_id=1, source_target_pairs={{32,0},{33,1},{34,2},{35,3},{36,4},{37,5},{38,6},{39,7},{40,8},{41... | collective-permute-start | bytes 2359304 | tf_op jit(solution)/shard_map/ppermute | solution.py:229
  68.0 1.3 %collective-permute-start.7 = (f32[32,6144]{1,0:T(8,128)}, f32[32,6144]{1,0:T(8,128)}, u32[]{:S(2)}, u32[]{:S(2)}) collective-permute-start(f32[32,6144]{1,0:T(8,128)} %collective-permute-done.2.even_ref.even2_ref), channel_id=1, source_target_pairs={{0,32},{1,33},{2,34},{3,35},{4,36},{5,37},{6,38},{7,39},{8,40},{9,... | collective-permute-start | bytes 2359304 | tf_op jit(solution)/shard_map/ppermute | solution.py:230
  69.2 1.2 %all-to-all-done.1.got_ref = f32[4,32,128]{2,1,0:T(8,128)S(1)} async-done(((f32[4,32,128]{2,1,0:T(8,128)}), f32[4,32,128]{2,1,0:T(8,128)S(1)}, u32[]{:S(2)}, u32[]{:S(2)}) %all-to-all-start.1) | async-done | bytes 65568 | tf_op jit(solution)/shard_map/all_to_all | solution.py:228
  70.5 0.1 shard_map.30.inter_ref
  70.6 1.8 %collective-permute-done.7.even3_ref = f32[32,6144]{1,0:T(8,128)} collective-permute-done((f32[32,6144]{1,0:T(8,128)}, f32[32,6144]{1,0:T(8,128)}, u32[]{:S(2)}, u32[]{:S(2)}) %collective-permute-start.7) | collective-permute-done | bytes 786464 | tf_op jit(solution)/shard_map/ppermute | solution.py:230
  72.5 3.4 %shard_map.31 = f32[32,6144]{1,0:T(8,128)} custom-call(s32[1]{0:T(128)} %bitcast.odd_ref, f32[32,128]{1,0:T(8,128)S(1)} %shard_map.30.inter_ref, f32[32,6144]{1,0:T(8,128)S(1)} %copy-done.1, f32[32,6144]{1,0:T(8,128)} %collective-permute-done.6.odd1_ref, f32[32,6144]{1,0:T(8,128)} %collective-permute-done.5.even1_ref, ...), custom_call_target="tpu_custom_call" | custom-call | tf_op jit(solution)/shard_map/pallas_call | solution.py:193
  (9 shorter events, 0.1 us)
Async XLA Ops:
  0.0 19.1 %copy-start = (f32[32,6144]{1,0:T(8,128)S(1)}, f32[32,6144]{1,0:T(8,128)}, u32[]{:S(2)}) copy-start(f32[32,6144]{1,0:T(8,128)} %h_ref.3) | copy-start | bytes 2359300
  0.0 19.1 %collective-permute-start.1 = (f32[32,6144]{1,0:T(8,128)}, f32[32,6144]{1,0:T(8,128)S(1)}, u32[]{:S(2)}, u32[]{:S(2)}) collective-permute-start(f32[32,6144]{1,0:T(8,128)} %psi_ref.1), channel_id=1, source_target_pairs={{32,96},{96,160},{160,224},{224,288},{288,352},{352,416},{416,480}... | collective-permute-start | bytes 2359304 | tf_op jit(solution)/shard_map/ppermute | solution.py:16
  4.3 17.2 %collective-permute-start = (f32[32,6144]{1,0:T(8,128)}, f32[32,6144]{1,0:T(8,128)S(1)}, u32[]{:S(2)}, u32[]{:S(2)}) collective-permute-start(f32[32,6144]{1,0:T(8,128)} %h_ref.3), channel_id=1, source_target_pairs={{0,992},{32,0},{64,32},{96,64},{128,96},{160,128},{192,160},{224,1... | collective-permute-start | bytes 2359304 | tf_op jit(solution)/shard_map/ppermute | solution.py:16
  18.7 1.1 %copy-start.1 = (f32[32,6144]{1,0:T(8,128)S(1)}, f32[32,6144]{1,0:T(8,128)}, u32[]{:S(2)}) copy-start(f32[32,6144]{1,0:T(8,128)} %psi_ref.1) | copy-start | bytes 2359300
  19.9 15.0 %collective-permute-start.2 = (f32[32,6144]{1,0:T(8,128)S(1)}, f32[32,6144]{1,0:T(8,128)}, u32[]{:S(2)}, u32[]{:S(2)}) collective-permute-start(f32[32,6144]{1,0:T(8,128)S(1)} %copy-done.1), channel_id=1, source_target_pairs={{0,64},{64,128},{128,192},{192,256},{256,320},{320,384},{384,448},... | collective-permute-start | bytes 2359304 | tf_op jit(solution)/shard_map/ppermute | solution.py:16
  22.5 12.5 %collective-permute-start.3 = (f32[32,64]{1,0:T(8,128)S(1)}, f32[32,64]{1,0:T(8,128)S(1)}, u32[]{:S(2)}, u32[]{:S(2)}) collective-permute-start(f32[32,64]{1,0:T(8,128)S(1)} %pad_maximum_fusion), channel_id=1, source_target_pairs={{32,96},{96,160},{160,224},{224,288},{288,352},{352,416},{416,480}... | collective-permute-start | bytes 24584 | tf_op jit(solution)/shard_map/ppermute | solution.py:16
  35.7 14.3 %all-to-all-start = ((f32[16,16,128]{2,1,0:T(8,128)}), f32[16,16,128]{2,1,0:T(8,128)S(1)}, u32[]{:S(2)}, u32[]{:S(2)}) async-start(f32[16,16,128]{2,1,0:T(8,128)} %shard_map.28), calls=%async_computation | async-start | bytes 262144 | tf_op jit(solution)/shard_map/all_to_all | solution.py:223
  42.7 27.8 %collective-permute-start.4 = (f32[32,6144]{1,0:T(8,128)S(1)}, f32[32,6144]{1,0:T(8,128)S(1)}, u32[]{:S(2)}, u32[]{:S(2)}) collective-permute-start(f32[32,6144]{1,0:T(8,128)S(1)} %collective-permute-done.1.odd2_ref), channel_id=1, source_target_pairs={{32,64},{96,128},{160,192},{224,256},{288,320},{352,384},{416,448}... | collective-permute-start | bytes 2359304 | tf_op jit(solution)/shard_map/ppermute | solution.py:16
  44.0 26.5 %collective-permute-start.5 = (f32[32,6144]{1,0:T(8,128)S(1)}, f32[32,6144]{1,0:T(8,128)}, u32[]{:S(2)}, u32[]{:S(2)}) collective-permute-start(f32[32,6144]{1,0:T(8,128)S(1)} %copy-done.1), channel_id=1, source_target_pairs={{0,32},{1,33},{2,34},{3,35},{4,36},{5,37},{6,38},{7,39},{8,40},{9,... | collective-permute-start | bytes 2359304 | tf_op jit(solution)/shard_map/ppermute | solution.py:225
  50.7 19.8 %all-to-all-start.1 = ((f32[4,32,128]{2,1,0:T(8,128)}), f32[4,32,128]{2,1,0:T(8,128)S(1)}, u32[]{:S(2)}, u32[]{:S(2)}) async-start(f32[4,32,128]{2,1,0:T(8,128)} %shard_map.29), calls=%async_computation.1 | async-start | bytes 131072 | tf_op jit(solution)/shard_map/all_to_all | solution.py:228
  63.6 7.0 %collective-permute-start.6 = (f32[32,6144]{1,0:T(8,128)S(1)}, f32[32,6144]{1,0:T(8,128)}, u32[]{:S(2)}, u32[]{:S(2)}) collective-permute-start(f32[32,6144]{1,0:T(8,128)S(1)} %collective-permute-done.1.odd2_ref), channel_id=1, source_target_pairs={{32,0},{33,1},{34,2},{35,3},{36,4},{37,5},{38,6},{39,7},{40,8},{41... | collective-permute-start | bytes 2359304 | tf_op jit(solution)/shard_map/ppermute | solution.py:229
  68.0 4.5 %collective-permute-start.7 = (f32[32,6144]{1,0:T(8,128)}, f32[32,6144]{1,0:T(8,128)}, u32[]{:S(2)}, u32[]{:S(2)}) collective-permute-start(f32[32,6144]{1,0:T(8,128)} %collective-permute-done.2.even_ref.even2_ref), channel_id=1, source_target_pairs={{0,32},{1,33},{2,34},{3,35},{4,36},{5,37},{6,38},{7,39},{8,40},{9,... | collective-permute-start | bytes 2359304 | tf_op jit(solution)/shard_map/ppermute | solution.py:230

commit v6 on v5

--- a/solution.py
+++ b/solution.py
@@ -143,7 +143,7 @@
         in_specs=[SCALAR, VECTOR],
         out_specs=VECTOR,
         cost_estimate=pl.CostEstimate(
-            flops=8_000_000_000, bytes_accessed=1024, transcendentals=0
+            flops=100_000, bytes_accessed=1024, transcendentals=0
         ),
     )(odd, *near(got))
 
@@ -214,22 +214,20 @@
     even2 = shifted(psi_later, 2, 0, 2)
 
     ahead, ahead_odd = overlap(ahead1, psi), overlap(ahead1, odd2)
-    hopped = shifted(jnp.concatenate([ahead, ahead_odd], 1), 2, 1, 2)
+    even1 = lax.ppermute(psi, "core", [(0, 1)])
+    for_next, even1 = lax.optimization_barrier((jnp.concatenate([ahead, ahead_odd], 1), even1))
+    hopped = shifted(for_next, 2, 1, 2)
 
     slots = slots_of(
         odd, (hpsi, ahead1, even2), (own, ahead, own_odd, hopped), 2 * lax.axis_size("x")
     )
-    slots, odd2_later, psi_later = lax.optimization_barrier((slots, odd2, psi))
+    slots, odd2_later, even2_later = lax.optimization_barrier((slots, odd2, even2))
     got = lax.all_to_all(slots, ("core", "x"), 0, 0, tiled=True)
     odd3 = shifted(odd2_later, 1, 1, 2)
-    even1 = lax.ppermute(psi_later, "core", [(0, 1)])
+    odd1 = lax.ppermute(odd2_later, "core", [(1, 0)])
+    even3 = lax.ppermute(even2_later, "core", [(0, 1)])
     line = line_of(got, lax.axis_size("zh"))
-    line, odd2_last, even2_last = lax.optimization_barrier((line, odd2, even2))
     got = lax.all_to_all(line, "zh", 0, 0, tiled=True)
-    odd1 = lax.ppermute(odd2_last, "core", [(1, 0)])
-    even3 = lax.ppermute(even2_last, "core", [(0, 1)])
-    got, odd3 = lax.optimization_barrier((got, odd3))
-    got, even1 = lax.optimization_barrier((got, even1))
     inter = total_of(odd, got)
     return finished(odd, inter, (psi, odd1, even1, odd2, even2, odd3, even3), hpsi)
 

time: 76.4 us -> 77.6 us (1.016)
  blocking collectives: 0 us -> 20.8 us
  starting transfers between devices: 48.5 us -> 37.7 us
  waiting for transfers between devices: 18.7 us -> 9.24 us
  local copies, waits for them, and re-layouts: 0.27 us -> 1.52 us
    all_to_all x0 -> x1, blocking collectives: none -> 20.8 us  [on_device(): got = lax.all_to_all(line, 'zh', 0, 0, tiled=True)]
    all_to_all x1 -> x0, starting transfers between devices: 12.9 us -> none  [on_device(): got = lax.all_to_all(line, 'zh', 0, 0, tiled=True)]
    all_to_all x1, waiting for transfers between devices: 4.72 us -> 0.01 us  [on_device(): got = lax.all_to_all(slots, ('core', 'x'), 0, 0, tiled=True)]
    ppermute x3, waiting for transfers between devices: 1.85 us -> 0.01 us  [the longest x1 0.01 us: on_device(): even1 = lax.ppermute(psi, 'core', [(0, 1)])]
    ppermute x5, waiting for transfers between devices: 10.9 us -> 9.23 us  [shifted(): return lax.ppermute(value, BAND, pairs)]
    all_to_all x1, starting transfers between devices: 6.97 us -> 8.55 us  [on_device(): got = lax.all_to_all(slots, ('core', 'x'), 0, 0, tiled=True)]
    unnamed x4 -> x8, local copies, waits for them, and re-layouts: 0.27 us -> 1.52 us
    all_to_all x1 -> x0, waiting for transfers between devices: 1.23 us -> none  [on_device(): got = lax.all_to_all(line, 'zh', 0, 0, tiled=True)]
  transfers between devices with their start and end apart: 10 -> 9, of which waited for: 5 -> 1; matrix products, arithmetic and copies ran while one was open for 4% -> 4% of each run, Pallas kernels for 1% -> 0%
where the time goes in v6:
time: 77.6 us; the launch traced here: 77.1 us
  starting transfers between devices  37.7 us (49%)
  blocking collectives  20.8 us (27%)
  waiting for transfers between devices  9.24 us (12%)
  Pallas kernels  4.29 us (6%)
  matrix products  3.23 us (4%)
  local copies, waits for them, and re-layouts  1.52 us (2%)
    ppermute x5, starting transfers between devices, shifted(): return lax.ppermute(value, BAND, pairs)  22.6 us
    all_to_all x1, blocking collectives, on_device(): got = lax.all_to_all(line, 'zh', 0, 0, tiled=True)  20.8 us
    ppermute x5, waiting for transfers between devices, shifted(): return lax.ppermute(value, BAND, pairs)  9.23 us
    all_to_all x1, starting transfers between devices, on_device(): got = lax.all_to_all(slots, ('core', 'x'), 0, 0, tiled=True)  8.55 us
    ppermute x1, starting transfers between devices, on_device(): odd1 = lax.ppermute(odd2_later, 'core', [(1, 0)])  3.83 us
    pallas_call x1, Pallas kernels, finished(): pl.pallas_call(finish_kernel, out_shape=jax.ShapeDtypeStruct(shape, jnp.f...  3.36 us
    dot_general x4, matrix products, overlap(): lax.dot_general(h, psi, (((1,), (1,)), ((), ())), precision=PRECISION, pr...  3.23 us
  transfers between devices with their start and end apart: 9, of which 1 were waited for; matrix products, arithmetic and copies ran while one was open for 4% of the time, Pallas kernels for 0%

profile of v6, /device:TPU:1, one launch (start us, length us, event | category | flops | bytes accessed | tf_op | source)
XLA Modules:
  0.0 77.1 jit_solution(15623576226544914546)
XLA Ops:
  0.0 4.3 %collective-permute-start.1 = (f32[32,6144]{1,0:T(8,128)}, f32[32,6144]{1,0:T(8,128)S(1)}, u32[]{:S(2)}, u32[]{:S(2)}) collective-permute-start(f32[32,6144]{1,0:T(8,128)} %psi_ref.1), channel_id=1, source_target_pairs={{32,96},{96,160},{160,224},{224,288},{288,352},{352,416},{416,480}... | collective-permute-start | bytes 2359304 | tf_op jit(solution)/shard_map/ppermute | solution.py:16
  4.3 12.6 %collective-permute-start = (f32[32,6144]{1,0:T(8,128)}, f32[32,6144]{1,0:T(8,128)S(1)}, u32[]{:S(2)}, u32[]{:S(2)}) collective-permute-start(f32[32,6144]{1,0:T(8,128)} %h_ref.3), channel_id=1, source_target_pairs={{0,992},{32,0},{64,32},{96,64},{128,96},{160,128},{192,160},{224,1... | collective-permute-start | bytes 2359304 | tf_op jit(solution)/shard_map/ppermute | solution.py:16
  16.9 1.3 %collective-permute-start.3 = (f32[32,6144]{1,0:T(8,128)}, f32[32,6144]{1,0:T(8,128)S(1)}, u32[]{:S(2)}, u32[]{:S(2)}) collective-permute-start(f32[32,6144]{1,0:T(8,128)} %psi_ref.1), channel_id=1, source_target_pairs={{0,32},{1,33},{2,34},{3,35},{4,36},{5,37},{6,38},{7,39},{8,40},{9,... | collective-permute-start | bytes 2359304 | tf_op jit(solution)/shard_map/ppermute | solution.py:217
  18.2 1.8 %fusion.own_ref = f32[32,32]{1,0:T(8,128)S(1)} fusion(f32[32,6144]{1,0:T(8,128)} %h_ref.3, f32[32,6144]{1,0:T(8,128)} %psi_ref.1), kind=kOutput, calls=%fused_computation.1 | convolution fusion | flops 37748736 | bytes 1576960 | tf_op jit(solution)/shard_map/dot_general | solution.py:20
  20.1 0.0 copy-start.1
  20.1 0.0 collective-permute-done.1.odd2_ref
  20.1 0.5 fusion.1.own_odd_ref
  20.6 0.6 copy-done.1
  21.2 1.6 %collective-permute-start.2 = (f32[32,6144]{1,0:T(8,128)S(1)}, f32[32,6144]{1,0:T(8,128)}, u32[]{:S(2)}, u32[]{:S(2)}) collective-permute-start(f32[32,6144]{1,0:T(8,128)S(1)} %copy-done.1), channel_id=1, source_target_pairs={{0,64},{64,128},{128,192},{192,256},{256,320},{320,384},{384,448},... | collective-permute-start | bytes 2359304 | tf_op jit(solution)/shard_map/ppermute | solution.py:16
  22.7 0.5 fusion.2.ahead_ref
  23.2 0.5 fusion.3
  23.7 0.1 pad_maximum_fusion
  23.8 0.0 collective-permute-done.3.even1_ref
  23.8 0.9 %copy-done.2 = f32[32,6144]{1,0:T(8,128)} copy-done((f32[32,6144]{1,0:T(8,128)}, f32[32,6144]{1,0:T(8,128)S(1)}, u32[]{:S(2)}) %copy-start.2) | copy-done | bytes 786456
  24.7 1.9 %collective-permute-start.4 = (f32[32,64]{1,0:T(8,128)S(1)}, f32[32,64]{1,0:T(8,128)S(1)}, u32[]{:S(2)}, u32[]{:S(2)}) collective-permute-start(f32[32,64]{1,0:T(8,128)S(1)} %pad_maximum_fusion), channel_id=1, source_target_pairs={{32,96},{96,160},{160,224},{224,288},{288,352},{352,416},{416,480}... | collective-permute-start | bytes 24584 | tf_op jit(solution)/shard_map/ppermute | solution.py:16
  26.6 9.2 %collective-permute-done.4.hop_ref = f32[32,64]{1,0:T(8,128)S(1)} collective-permute-done((f32[32,64]{1,0:T(8,128)S(1)}, f32[32,64]{1,0:T(8,128)S(1)}, u32[]{:S(2)}, u32[]{:S(2)}) %collective-permute-start.4) | collective-permute-done | bytes 8224 | tf_op jit(solution)/shard_map/ppermute | solution.py:16
  35.8 0.8 shard_map.28
  36.6 8.5 %all-to-all-start = ((f32[16,16,128]{2,1,0:T(8,128)}), f32[16,16,128]{2,1,0:T(8,128)S(1)}, u32[]{:S(2)}, u32[]{:S(2)}) async-start(f32[16,16,128]{2,1,0:T(8,128)} %shard_map.28), calls=%async_computation | async-start | bytes 262144 | tf_op jit(solution)/shard_map/all_to_all | solution.py:225
  45.1 1.4 %collective-permute-start.7 = (f32[32,6144]{1,0:T(8,128)}, f32[32,6144]{1,0:T(8,128)}, u32[]{:S(2)}, u32[]{:S(2)}) collective-permute-start(f32[32,6144]{1,0:T(8,128)} %collective-permute-done.2.even_ref.even2_ref), channel_id=1, source_target_pairs={{0,32},{1,33},{2,34},{3,35},{4,36},{5,37},{6,38},{7,39},{8,40},{9,... | collective-permute-start | bytes 2359304 | tf_op jit(solution)/shard_map/ppermute | solution.py:228
  46.6 2.3 %collective-permute-start.6 = (f32[32,6144]{1,0:T(8,128)S(1)}, f32[32,6144]{1,0:T(8,128)}, u32[]{:S(2)}, u32[]{:S(2)}) collective-permute-start(f32[32,6144]{1,0:T(8,128)S(1)} %collective-permute-done.1.odd2_ref), channel_id=1, source_target_pairs={{32,64},{96,128},{160,192},{224,256},{288,320},{352,384},{416,448}... | collective-permute-start | bytes 2359304 | tf_op jit(solution)/shard_map/ppermute | solution.py:16
  48.9 3.8 %collective-permute-start.5 = (f32[32,6144]{1,0:T(8,128)S(1)}, f32[32,6144]{1,0:T(8,128)}, u32[]{:S(2)}, u32[]{:S(2)}) collective-permute-start(f32[32,6144]{1,0:T(8,128)S(1)} %collective-permute-done.1.odd2_ref), channel_id=1, source_target_pairs={{32,0},{33,1},{34,2},{35,3},{36,4},{37,5},{38,6},{39,7},{40,8},{41... | collective-permute-start | bytes 2359304 | tf_op jit(solution)/shard_map/ppermute | solution.py:227
  52.7 20.8 %all_to_all.10.got_ref = f32[4,32,128]{2,1,0:T(8,128)S(1)} all-to-all(f32[4,32,128]{2,1,0:T(8,128)S(1)} %shard_map.29), channel_id=1, replica_groups=mesh['zl'=2,'y'=8,'core'=2,'zh'=4,'x'=8] {'zh'}, dimensions={0} | all-to-all | bytes 131072 | tf_op jit(solution)/shard_map/all_to_all | solution.py:230
  73.5 0.1 shard_map.30.inter_ref
  73.7 3.4 %shard_map.31 = f32[32,6144]{1,0:T(8,128)} custom-call(s32[1]{0:T(128)} %bitcast.odd_ref, f32[32,128]{1,0:T(8,128)S(1)} %shard_map.30.inter_ref, f32[32,6144]{1,0:T(8,128)S(1)} %copy-done.1, f32[32,6144]{1,0:T(8,128)} %collective-permute-done.5.odd1_ref, f32[32,6144]{1,0:T(8,128)S(1)} %copy-done.3, f32[32,6144]{1,0:T(8,128)S(1)} %collective-permute-done.1.odd2_ref, ...), custom_call_target="tpu_custom_call" | custom-call | tf_op jit(solution)/shard_map/pallas_call | solution.py:193
  (12 shorter events, 0.0 us)
Async XLA Ops:
  0.0 20.1 %copy-start = (f32[32,6144]{1,0:T(8,128)S(1)}, f32[32,6144]{1,0:T(8,128)}, u32[]{:S(2)}) copy-start(f32[32,6144]{1,0:T(8,128)} %h_ref.3) | copy-start | bytes 2359300
  0.0 20.1 %collective-permute-start.1 = (f32[32,6144]{1,0:T(8,128)}, f32[32,6144]{1,0:T(8,128)S(1)}, u32[]{:S(2)}, u32[]{:S(2)}) collective-permute-start(f32[32,6144]{1,0:T(8,128)} %psi_ref.1), channel_id=1, source_target_pairs={{32,96},{96,160},{160,224},{224,288},{288,352},{352,416},{416,480}... | collective-permute-start | bytes 2359304 | tf_op jit(solution)/shard_map/ppermute | solution.py:16
  4.3 18.5 %collective-permute-start = (f32[32,6144]{1,0:T(8,128)}, f32[32,6144]{1,0:T(8,128)S(1)}, u32[]{:S(2)}, u32[]{:S(2)}) collective-permute-start(f32[32,6144]{1,0:T(8,128)} %h_ref.3), channel_id=1, source_target_pairs={{0,992},{32,0},{64,32},{96,64},{128,96},{160,128},{192,160},{224,1... | collective-permute-start | bytes 2359304 | tf_op jit(solution)/shard_map/ppermute | solution.py:16
  16.9 6.9 %collective-permute-start.3 = (f32[32,6144]{1,0:T(8,128)}, f32[32,6144]{1,0:T(8,128)S(1)}, u32[]{:S(2)}, u32[]{:S(2)}) collective-permute-start(f32[32,6144]{1,0:T(8,128)} %psi_ref.1), channel_id=1, source_target_pairs={{0,32},{1,33},{2,34},{3,35},{4,36},{5,37},{6,38},{7,39},{8,40},{9,... | collective-permute-start | bytes 2359304 | tf_op jit(solution)/shard_map/ppermute | solution.py:217
  20.1 1.1 %copy-start.1 = (f32[32,6144]{1,0:T(8,128)S(1)}, f32[32,6144]{1,0:T(8,128)}, u32[]{:S(2)}) copy-start(f32[32,6144]{1,0:T(8,128)} %psi_ref.1) | copy-start | bytes 2359300
  21.2 14.6 %collective-permute-start.2 = (f32[32,6144]{1,0:T(8,128)S(1)}, f32[32,6144]{1,0:T(8,128)}, u32[]{:S(2)}, u32[]{:S(2)}) collective-permute-start(f32[32,6144]{1,0:T(8,128)S(1)} %copy-done.1), channel_id=1, source_target_pairs={{0,64},{64,128},{128,192},{192,256},{256,320},{320,384},{384,448},... | collective-permute-start | bytes 2359304 | tf_op jit(solution)/shard_map/ppermute | solution.py:16
  23.8 0.9 %copy-start.2 = (f32[32,6144]{1,0:T(8,128)}, f32[32,6144]{1,0:T(8,128)S(1)}, u32[]{:S(2)}) copy-start(f32[32,6144]{1,0:T(8,128)S(1)} %collective-permute-done.3.even1_ref) | copy-start | bytes 2359300
  24.7 11.1 %collective-permute-start.4 = (f32[32,64]{1,0:T(8,128)S(1)}, f32[32,64]{1,0:T(8,128)S(1)}, u32[]{:S(2)}, u32[]{:S(2)}) collective-permute-start(f32[32,64]{1,0:T(8,128)S(1)} %pad_maximum_fusion), channel_id=1, source_target_pairs={{32,96},{96,160},{160,224},{224,288},{288,352},{352,416},{416,480}... | collective-permute-start | bytes 24584 | tf_op jit(solution)/shard_map/ppermute | solution.py:16
  36.6 16.1 %all-to-all-start = ((f32[16,16,128]{2,1,0:T(8,128)}), f32[16,16,128]{2,1,0:T(8,128)S(1)}, u32[]{:S(2)}, u32[]{:S(2)}) async-start(f32[16,16,128]{2,1,0:T(8,128)} %shard_map.28), calls=%async_computation | async-start | bytes 262144 | tf_op jit(solution)/shard_map/all_to_all | solution.py:225
  45.1 28.6 %copy-start.3 = (f32[32,6144]{1,0:T(8,128)S(1)}, f32[32,6144]{1,0:T(8,128)}, u32[]{:S(2)}) copy-start(f32[32,6144]{1,0:T(8,128)} %copy-done.2) | copy-start | bytes 2359300
  45.1 28.5 %collective-permute-start.7 = (f32[32,6144]{1,0:T(8,128)}, f32[32,6144]{1,0:T(8,128)}, u32[]{:S(2)}, u32[]{:S(2)}) collective-permute-start(f32[32,6144]{1,0:T(8,128)} %collective-permute-done.2.even_ref.even2_ref), channel_id=1, source_target_pairs={{0,32},{1,33},{2,34},{3,35},{4,36},{5,37},{6,38},{7,39},{8,40},{9,... | collective-permute-start | bytes 2359304 | tf_op jit(solution)/shard_map/ppermute | solution.py:228
  46.6 27.1 %collective-permute-start.6 = (f32[32,6144]{1,0:T(8,128)S(1)}, f32[32,6144]{1,0:T(8,128)}, u32[]{:S(2)}, u32[]{:S(2)}) collective-permute-start(f32[32,6144]{1,0:T(8,128)S(1)} %collective-permute-done.1.odd2_ref), channel_id=1, source_target_pairs={{32,64},{96,128},{160,192},{224,256},{288,320},{352,384},{416,448}... | collective-permute-start | bytes 2359304 | tf_op jit(solution)/shard_map/ppermute | solution.py:16
  48.9 24.8 %collective-permute-start.5 = (f32[32,6144]{1,0:T(8,128)S(1)}, f32[32,6144]{1,0:T(8,128)}, u32[]{:S(2)}, u32[]{:S(2)}) collective-permute-start(f32[32,6144]{1,0:T(8,128)S(1)} %collective-permute-done.1.odd2_ref), channel_id=1, source_target_pairs={{32,0},{33,1},{34,2},{35,3},{36,4},{37,5},{38,6},{39,7},{40,8},{41... | collective-permute-start | bytes 2359304 | tf_op jit(solution)/shard_map/ppermute | solution.py:227
